TPU v7x, 32 devices: a whole 2x2x4 slice. The times are simulated.
32 devices in a mesh: edata: 4 (over x, core), expert: 8 (over z, y).
Axes of the slice: x: 2, y: 2, z: 4, core: 2. Of those that a mesh axis runs over, the one named last changes fastest.
Arguments:
- tokens_one: bfloat16 [512, 3584], P(('edata', 'expert')), may hold values from -6 to 6
- routes_one: int32 [512, 2], P(('edata', 'expert')), may hold values from 0 to 7, all different within a row; in each aligned block of 16 rows (0 to 15, 16 to 31, ...) at most 5 rows name the same one
- gates_one: float32 [512, 2], P(('edata', 'expert')), may hold values from 0.2 to 1
- tokens_two: bfloat16 [512, 3584], P(('edata', 'expert')), may hold values from -6 to 6
- routes_two: int32 [512, 2], P(('edata', 'expert')), may hold values from 0 to 7, all different within a row; in each aligned block of 16 rows (0 to 15, 16 to 31, ...) at most 5 rows name the same one
- gates_two: float32 [512, 2], P(('edata', 'expert')), may hold values from 0.2 to 1
- cot_two: bfloat16 [512, 3584], P(('edata', 'expert')), may hold values from -6 to 6
- rows_three: bfloat16 [1024, 3584], P(('edata', 'expert')), may hold values from -6 to 6
- cot_three: bfloat16 [1024, 3584], P(('edata', 'expert')), may hold values from -0.29882812 to 0.29882812
- w_gate: bfloat16 [3584, 1024], P(None, 'expert'), may hold values from -0.09375 to 0.09375
- w_up: bfloat16 [3584, 1024], P(None, 'expert'), may hold values from -0.09375 to 0.09375
- w_down: bfloat16 [1024, 3584], P('expert'), may hold values from -0.5 to 0.5
Outputs:
- out_one: bfloat16 [512, 3584], P(('edata', 'expert'))
- dx_two: bfloat16 [512, 3584], P(('edata', 'expert'))
- weight_grads: bfloat16 [3584, 3, 1024], P('edata', None, 'expert')
Inputs may be any that keep to these rules, and one draw needn't show every extreme that they name: `routes_one`: each row names 2 different experts; among the rows of one device no expert is named more than 5 times, and that count is reached. `routes_two`: each row names 2 different experts; among the rows of one device no expert is named more than 5 times, and that count is reached.
All inputs are finite; a program needn't handle non-finite values.
Results may differ from a plain program's by a relative error of at most 0.009.
Values may be sent and summed in bfloat16 or wider, within the bound.
A program may use at most 64 MiB of HBM per device.

v0:
```python
import jax
import jax.numpy as jnp
from jax import lax
from jax.sharding import PartitionSpec as P

EXPERTS = 8
TOP = 2
CAP = 5


def forward_factors(block_rows, slice_gate, slice_up):
    gate_pre = jnp.dot(block_rows, slice_gate, preferred_element_type=jnp.float32)
    up_pre = jnp.dot(block_rows, slice_up, preferred_element_type=jnp.float32)
    gate_sigma = jax.nn.sigmoid(gate_pre)
    hidden = (gate_pre * gate_sigma * up_pre).astype(jnp.bfloat16)
    return (gate_pre, up_pre, gate_sigma, hidden)


def backward_factors(block_cot, slice_down, gate_pre, up_pre, gate_sigma):
    d_hidden = lax.dot_general(
        block_cot, slice_down, (((1,), (1,)), ((), ())), preferred_element_type=jnp.float32
    )
    d_gate = (d_hidden * up_pre * gate_sigma * (1.0 + gate_pre * (1.0 - gate_sigma))).astype(
        jnp.bfloat16
    )
    d_up = (d_hidden * gate_pre * gate_sigma).astype(jnp.bfloat16)
    return (d_gate, d_up)


def transpose_product(factor, weights):
    return lax.dot_general(
        factor, weights, (((1,), (1,)), ((), ())), preferred_element_type=jnp.float32
    )


def column_window(matrix, factor):
    return lax.dot_general(
        matrix, factor, (((0,), (0,)), ((), ())), preferred_element_type=jnp.float32
    )


def placement_matrix(routes):
    route_list = routes.reshape(-1)
    expert_ids = lax.broadcasted_iota(jnp.int32, (1, EXPERTS), 1)
    onehot = (route_list[:, None] == expert_ids).astype(jnp.int32)
    position = jnp.sum((jnp.cumsum(onehot, axis=0) - onehot) * onehot, axis=1)
    target = route_list * CAP + position
    slot_ids = lax.broadcasted_iota(jnp.int32, (EXPERTS * CAP, 1), 0)
    return (target[None, :] == slot_ids).astype(jnp.bfloat16)


def shards(
    tokens_one,
    routes_one,
    gates_one,
    tokens_two,
    routes_two,
    gates_two,
    cot_two,
    rows_three,
    cot_three,
    w_gate,
    w_up,
    w_down,
):
    experts_axis = lax.axis_size("expert")
    slice_count = experts_axis // EXPERTS
    row_width = tokens_one.shape[1]

    def forward_work(stacked):
        gate_pre, up_pre, gate_sigma, hidden = forward_factors(stacked[0], w_gate, w_up)
        return jnp.dot(hidden, w_down, preferred_element_type=jnp.float32).astype(jnp.bfloat16)

    def backward_work(stacked):
        gate_pre, up_pre, gate_sigma, hidden = forward_factors(stacked[0], w_gate, w_up)
        d_gate, d_up = backward_factors(stacked[1], w_down, gate_pre, up_pre, gate_sigma)
        return (transpose_product(d_gate, w_gate) + transpose_product(d_up, w_up)).astype(
            jnp.bfloat16
        )

    def dispatch(buffers, work):
        stacked = jnp.stack(buffers, axis=0)
        stack_depth = stacked.shape[0]
        grouped = stacked.reshape(stack_depth, EXPERTS, 1, CAP, row_width)
        outgoing = jnp.broadcast_to(
            grouped, (stack_depth, EXPERTS, slice_count, CAP, row_width)
        ).reshape(stack_depth, experts_axis, CAP, row_width)
        arrived = lax.all_to_all(outgoing, "expert", split_axis=1, concat_axis=1, tiled=True)
        slot_count = arrived.shape[2]
        partial_value = work(arrived.reshape(stack_depth, experts_axis * slot_count, row_width))
        answer = lax.all_to_all(
            partial_value.reshape(experts_axis, slot_count, row_width),
            "expert",
            split_axis=0,
            concat_axis=0,
            tiled=True,
        )
        summed = jnp.sum(
            answer.reshape(EXPERTS, slice_count, CAP, row_width).astype(jnp.float32), axis=1
        )
        summed = summed.reshape(EXPERTS * CAP, row_width)
        return summed

    def gather_routes(placement, summed, weighting):
        weighted = placement.astype(jnp.float32) * weighting
        per_route = lax.dot_general(
            weighted,
            summed,
            (((0,), (0,)), ((), ())),
            precision=lax.Precision.HIGHEST,
            preferred_element_type=jnp.float32,
        )
        return jnp.sum(per_route.reshape(-1, TOP, row_width), axis=1).astype(jnp.bfloat16)

    placement = placement_matrix(routes_one)
    repeated = jnp.repeat(tokens_one, TOP, axis=0)
    buffer = jnp.dot(placement, repeated, preferred_element_type=jnp.float32).astype(jnp.bfloat16)
    summed = dispatch((buffer,), forward_work)
    out_one = gather_routes(placement, summed, gates_one.reshape(1, -1))
    placement = placement_matrix(routes_two)
    repeated = jnp.repeat(tokens_two, TOP, axis=0)
    scaled = (
        gates_two.reshape(-1, 1) * jnp.repeat(cot_two, TOP, axis=0).astype(jnp.float32)
    ).astype(jnp.bfloat16)
    row_buffer = jnp.dot(placement, repeated, preferred_element_type=jnp.float32).astype(
        jnp.bfloat16
    )
    cot_buffer = jnp.dot(placement, scaled, preferred_element_type=jnp.float32).astype(jnp.bfloat16)
    summed = dispatch((row_buffer, cot_buffer), backward_work)
    dx_two = gather_routes(placement, summed, 1.0)
    gate_pre, up_pre, gate_sigma, hidden = forward_factors(rows_three, w_gate, w_up)
    d_gate, d_up = backward_factors(cot_three, w_down, gate_pre, up_pre, gate_sigma)
    weight_grads = lax.psum_scatter(
        jnp.stack(
            [
                column_window(rows_three, d_gate),
                column_window(rows_three, d_up),
                column_window(cot_three, hidden),
            ],
            axis=1,
        ).astype(jnp.bfloat16),
        "edata",
        scatter_dimension=0,
        tiled=True,
    )
    return (out_one, dx_two, weight_grads)


def solution(mesh):
    return jax.shard_map(
        shards,
        mesh=mesh,
        in_specs=(
            P(("edata", "expert"), None),
            P(("edata", "expert"), None),
            P(("edata", "expert"), None),
            P(("edata", "expert"), None),
            P(("edata", "expert"), None),
            P(("edata", "expert"), None),
            P(("edata", "expert"), None),
            P(("edata", "expert"), None),
            P(("edata", "expert"), None),
            P(None, "expert"),
            P(None, "expert"),
            P("expert", None),
        ),
        out_specs=(
            P(("edata", "expert"), None),
            P(("edata", "expert"), None),
            P("edata", None, "expert"),
        ),
        check_vma=False,
    )
```

profile of v0, /device:TPU:0, one launch (start us, length us, event | category | flops | bytes accessed | tf_op | source)
XLA Modules:
  0.0 106.7 jit_solution(6286719956891511622)
XLA Ops:
  7.2 1.7 %fusion.50 = f32[32,128]{1,0:T(8,128)S(1)} fusion(bf16[32,3584]{1,0:T(8,128)(2,1)} %param.19, bf16[3584,128]{1,0:T(8,128)(2,1)} %param.21), kind=kOutput, calls=%fused_computation.83 | convolution fusion | flops 29360128 | bytes 1163264 | tf_op jit(solution)/shard_map/dot_general | solution.py:12
  8.9 1.2 %fusion.49 = f32[32,128]{1,0:T(8,128)S(1)} fusion(bf16[32,3584]{1,0:T(8,128)(2,1)} %param.19, bf16[3584,128]{1,0:T(8,128)(2,1)S(1)} %copy-done), kind=kOutput, calls=%fused_computation.82 | convolution fusion | flops 29360128 | bytes 1163264 | tf_op jit(solution)/shard_map/dot_general | solution.py:13
  10.1 1.7 %fusion.48 = f32[32,128]{1,0:T(8,128)S(1)} fusion(bf16[32,3584]{1,0:T(8,128)(2,1)} %param.20, bf16[128,3584]{1,0:T(8,128)(2,1)} %param.23), kind=kOutput, calls=%fused_computation.81 | convolution fusion | flops 29360128 | bytes 1163264 | tf_op jit(solution)/shard_map/dot_general | solution.py:20
  13.2 1.9 %pad_maximum_fusion = bf16[3584,3,128]{0,2,1:T(8,128)(2,1)} fusion(bf16[3584,1,128]{0,2,1:T(8,128)(2,1)S(1)} %fusion.2, bf16[3584,1,128]{0,2,1:T(8,128)(2,1)S(1)} %fusion.1, bf16[3584,1,128]{0,2,1:T(8,128)(2,1)S(1)} %fusion), kind=kLoop, calls=%fused_computation.12 | loop fusion | flops 2752512 | bytes 5505024 | tf_op jit(solution)/shard_map/stack | solution.py:134
  15.1 4.5 %copy.57 = bf16[3584,384]{1,0:T(8,128)(2,1)} copy(bf16[3584,384]{0,1:T(8,128)(2,1)} %bitcast.50) | data formatting | bytes 5505024
  19.6 0.6 copy-done.10
  21.2 0.9 reshape_reshape_stack.3
  22.1 7.3 %all-to-all-start = ((bf16[1,8,5,3584]{3,2,0,1:T(8,128)(2,1)}), bf16[1,8,5,3584]{3,2,0,1:T(8,128)(2,1)S(1)}, u32[]{:S(2)}, u32[]{:S(2)}) async-start(bf16[1,8,5,3584]{3,2,0,1:T(8,128)(2,1)} %bitcast.1), calls=%async_computation | async-start | bytes 917504 | tf_op jit(solution)/shard_map/all_to_all | solution.py:88
  31.8 1.5 %copy.53 = bf16[2,8,5,3584]{3,0,2,1:T(2,128)(2,1)} copy(bf16[2,8,5,3584]{3,2,1,0:T(8,128)(2,1)S(1)} %pad_maximum_fusion.1) | data formatting | bytes 1146880 | tf_op jit(solution)/shard_map/stack | solution.py:82
  33.3 9.2 %all-to-all-done = bf16[1,8,5,3584]{3,2,0,1:T(8,128)(2,1)S(1)} async-done(((bf16[1,8,5,3584]{3,2,0,1:T(8,128)(2,1)}), bf16[1,8,5,3584]{3,2,0,1:T(8,128)(2,1)S(1)}, u32[]{:S(2)}, u32[]{:S(2)}) %all-to-all-start) | async-done | bytes 286752 | tf_op jit(solution)/shard_map/all_to_all | solution.py:88
  42.5 0.8 copy-done.4
  43.3 3.6 %all-to-all-start.2 = ((bf16[2,8,5,3584]{3,0,2,1:T(2,128)(2,1)}), bf16[2,8,5,3584]{3,0,2,1:T(2,128)(2,1)S(1)}, u32[]{:S(2)}, u32[]{:S(2)}) async-start(bf16[2,8,5,3584]{3,0,2,1:T(2,128)(2,1)} %copy.53), calls=%async_computation.2 | async-start | bytes 1146880 | tf_op jit(solution)/shard_map/all_to_all | solution.py:88
  47.3 1.9 %squeeze_reshape.3 = bf16[40,3584]{1,0:T(8,128)(2,1)} reshape(bf16[1,8,5,3584]{3,2,0,1:T(8,128)(2,1)} %copy-done.4) | data formatting | bytes 573440 | tf_op jit(solution)/shard_map/squeeze;reshape | solution.py:71
  49.2 1.2 %fusion.45 = f32[40,128]{1,0:T(8,128)S(1)} fusion(bf16[40,3584]{1,0:T(8,128)(2,1)} %squeeze_reshape.3, bf16[3584,128]{1,0:T(8,128)(2,1)S(1)} %copy-done.1), kind=kOutput, calls=%fused_computation.78 | convolution fusion | flops 36700160 | bytes 1224704 | tf_op jit(solution)/shard_map/dot_general | solution.py:12
  50.4 2.2 %convolution_convert_fusion.5 = bf16[40,3584]{1,0:T(8,128)(2,1)} fusion(bf16[128,3584]{1,0:T(8,128)(2,1)S(1)} %copy-done.2, bf16[40,3584]{1,0:T(8,128)(2,1)} %squeeze_reshape.3, bf16[3584,128]{1,0:T(8,128)(2,1)S(1)} %copy-done, f32[40,128]{1,0:T(8,128)S(1)} %fusion.45), kind=kOutput, calls=%fused_computation.10 | convolution fusion | flops 73574400 | bytes 2428928 | tf_op jit(solution)/shard_map/dot_general | solution.py:72
  52.6 1.9 %reshape.121 = bf16[8,5,3584]{2,1,0:T(8,128)(2,1)} reshape(bf16[40,3584]{1,0:T(8,128)(2,1)} %convolution_convert_fusion.5) | data formatting | bytes 573440 | tf_op jit(solution)/shard_map/reshape | solution.py:92
  54.5 8.1 %all-to-all-done.2 = bf16[2,8,5,3584]{3,0,2,1:T(2,128)(2,1)S(1)} async-done(((bf16[2,8,5,3584]{3,0,2,1:T(2,128)(2,1)}), bf16[2,8,5,3584]{3,0,2,1:T(2,128)(2,1)S(1)}, u32[]{:S(2)}, u32[]{:S(2)}) %all-to-all-start.2) | async-done | bytes 573472 | tf_op jit(solution)/shard_map/all_to_all | solution.py:88
  62.6 4.1 %all-to-all-start.1 = ((bf16[8,5,3584]{2,1,0:T(8,128)(2,1)}), bf16[8,5,3584]{2,1,0:T(8,128)(2,1)}, u32[]{:S(2)}, u32[]{:S(2)}) async-start(bf16[8,5,3584]{2,1,0:T(8,128)(2,1)} %reshape.121), calls=%async_computation.1 | async-start | bytes 917504 | tf_op jit(solution)/shard_map/all_to_all | solution.py:91
  66.7 3.4 %slice_reduce_fusion = (bf16[8,5,3584]{2,1,0:T(8,128)(2,1)}, bf16[8,5,3584]{2,1,0:T(8,128)(2,1)}) fusion(bf16[2,8,5,3584]{3,0,2,1:T(2,128)(2,1)S(1)} %all-to-all-done.2), kind=kLoop, calls=%fused_computation.23 | loop fusion | bytes 1146880 | tf_op jit(solution)/shard_map/slice | solution.py:75
  70.1 1.1 %squeeze.7 = bf16[40,3584]{1,0:T(8,128)(2,1)S(1)} reshape(bf16[8,5,3584]{2,1,0:T(8,128)(2,1)} %get-tuple-element.15) | data formatting | bytes 573440 | tf_op jit(solution)/shard_map/squeeze | solution.py:75
  71.3 1.1 %squeeze.6 = bf16[40,3584]{1,0:T(8,128)(2,1)S(1)} reshape(bf16[8,5,3584]{2,1,0:T(8,128)(2,1)} %get-tuple-element.16) | data formatting | bytes 573440 | tf_op jit(solution)/shard_map/squeeze | solution.py:76
  73.1 0.9 fusion.8
  74.0 0.7 fusion.3
  74.6 0.9 reshape.125
  75.5 4.1 %all-to-all-done.1 = bf16[8,5,3584]{2,1,0:T(8,128)(2,1)} async-done(((bf16[8,5,3584]{2,1,0:T(8,128)(2,1)}), bf16[8,5,3584]{2,1,0:T(8,128)(2,1)}, u32[]{:S(2)}, u32[]{:S(2)}) %all-to-all-start.1) | async-done | bytes 286752 | tf_op jit(solution)/shard_map/all_to_all | solution.py:91
  79.6 3.6 %all-to-all-start.3 = ((bf16[8,5,3584]{2,1,0:T(8,128)(2,1)}), bf16[8,5,3584]{2,1,0:T(8,128)(2,1)S(1)}, u32[]{:S(2)}, u32[]{:S(2)}) async-start(bf16[8,5,3584]{2,1,0:T(8,128)(2,1)} %reshape.125), calls=%async_computation.3 | async-start | bytes 917504 | tf_op jit(solution)/shard_map/all_to_all | solution.py:91
  83.3 1.1 %reshape.127 = bf16[40,3584,1]{1,0,2:T(8,128)(2,1)S(1)} reshape(bf16[8,5,3584]{2,1,0:T(8,128)(2,1)} %all-to-all-done.1) | data formatting | bytes 573440 | tf_op jit(solution)/shard_map/reshape | solution.py:101
  84.4 1.1 convolution_reduce_fusion.1
  85.5 10.7 %all-to-all-done.3 = bf16[8,5,3584]{2,1,0:T(8,128)(2,1)S(1)} async-done(((bf16[8,5,3584]{2,1,0:T(8,128)(2,1)}), bf16[8,5,3584]{2,1,0:T(8,128)(2,1)S(1)}, u32[]{:S(2)}, u32[]{:S(2)}) %all-to-all-start.3) | async-done | bytes 286752 | tf_op jit(solution)/shard_map/all_to_all | solution.py:91
  96.3 0.9 convolution_reduce_fusion
  97.2 1.4 %copy.58 = bf16[896,384]{0,1:T(8,128)(2,1)S(1)} copy(bf16[896,384]{1,0:T(8,128)(2,1)} %reduce-scatter.4.cloned.1.call-done) | data formatting | bytes 1376256
  98.7 1.1 %copy.54 = bf16[896,3,128]{2,0,1:T(8,128)(2,1)} copy(bf16[896,3,128]{0,2,1:T(8,128)(2,1)S(1)} %bitcast.51) | data formatting | bytes 1376256
  (65 shorter events, 5.8 us)
Async XLA Ops:
  7.2 1.8 %copy-start = (bf16[3584,128]{1,0:T(8,128)(2,1)S(1)}, bf16[3584,128]{1,0:T(8,128)(2,1)}, u32[]{:S(2)}) copy-start(bf16[3584,128]{1,0:T(8,128)(2,1)} %param.22) | copy-start | bytes 2752516
  7.2 5.1 %copy-start.3 = (bf16[32,3584]{1,0:T(8,128)(2,1)S(1)}, bf16[32,3584]{1,0:T(8,128)(2,1)}, u32[]{:S(2)}) copy-start(bf16[32,3584]{1,0:T(8,128)(2,1)} %param.19) | copy-start | bytes 688132
  7.2 4.6 %copy-start.5 = (bf16[32,3584]{1,0:T(8,128)(2,1)S(1)}, bf16[32,3584]{1,0:T(8,128)(2,1)}, u32[]{:S(2)}) copy-start(bf16[32,3584]{1,0:T(8,128)(2,1)} %param.20) | copy-start | bytes 688132
  7.2 90.0 %reduce-scatter.4.cloned.1.call-start = ((), (), s32[]{:S(2)}) async-start(), calls=%async_computation.5 | async-start | bytes 3440640
  19.5 0.7 copy-start.10
  19.5 0.9 copy-start.6
  19.6 9.9 %copy-start.12 = (f32[16,2]{0,1:T(2,128)S(1)}, f32[16,2]{0,1:T(2,128)}, u32[]{:S(2)}) copy-start(f32[16,2]{0,1:T(2,128)} %param.17) | copy-start | bytes 388
  19.6 10.0 %copy-start.9 = (s32[16,2]{0,1:T(2,128)S(1)}, s32[16,2]{0,1:T(2,128)}, u32[]{:S(2)}) copy-start(s32[16,2]{0,1:T(2,128)} %param.16) | copy-start | bytes 388
  19.6 10.4 %copy-start.7 = (bf16[16,3584]{1,0:T(8,128)(2,1)S(1)}, bf16[16,3584]{1,0:T(8,128)(2,1)}, u32[]{:S(2)}) copy-start(bf16[16,3584]{1,0:T(8,128)(2,1)} %param.15) | copy-start | bytes 344068
  19.6 10.6 %copy-start.8 = (bf16[16,3584]{1,0:T(8,128)(2,1)S(1)}, bf16[16,3584]{1,0:T(8,128)(2,1)}, u32[]{:S(2)}) copy-start(bf16[16,3584]{1,0:T(8,128)(2,1)} %param.18) | copy-start | bytes 344068
  22.1 20.4 %all-to-all-start = ((bf16[1,8,5,3584]{3,2,0,1:T(8,128)(2,1)}), bf16[1,8,5,3584]{3,2,0,1:T(8,128)(2,1)S(1)}, u32[]{:S(2)}, u32[]{:S(2)}) async-start(bf16[1,8,5,3584]{3,2,0,1:T(8,128)(2,1)} %bitcast.1), calls=%async_computation | async-start | bytes 917504 | tf_op jit(solution)/shard_map/all_to_all | solution.py:88
  31.6 17.6 %copy-start.1 = (bf16[3584,128]{1,0:T(8,128)(2,1)S(1)}, bf16[3584,128]{1,0:T(8,128)(2,1)}, u32[]{:S(2)}) copy-start(bf16[3584,128]{1,0:T(8,128)(2,1)} %param.21) | copy-start | bytes 2752516
  31.8 18.6 %copy-start.2 = (bf16[128,3584]{1,0:T(8,128)(2,1)S(1)}, bf16[128,3584]{1,0:T(8,128)(2,1)}, u32[]{:S(2)}) copy-start(bf16[128,3584]{1,0:T(8,128)(2,1)} %param.23) | copy-start | bytes 2752516
  42.5 0.8 copy-start.4
  43.3 19.3 %all-to-all-start.2 = ((bf16[2,8,5,3584]{3,0,2,1:T(2,128)(2,1)}), bf16[2,8,5,3584]{3,0,2,1:T(2,128)(2,1)S(1)}, u32[]{:S(2)}, u32[]{:S(2)}) async-start(bf16[2,8,5,3584]{3,0,2,1:T(2,128)(2,1)} %copy.53), calls=%async_computation.2 | async-start | bytes 1146880 | tf_op jit(solution)/shard_map/all_to_all | solution.py:88
  62.6 17.1 %all-to-all-start.1 = ((bf16[8,5,3584]{2,1,0:T(8,128)(2,1)}), bf16[8,5,3584]{2,1,0:T(8,128)(2,1)}, u32[]{:S(2)}, u32[]{:S(2)}) async-start(bf16[8,5,3584]{2,1,0:T(8,128)(2,1)} %reshape.121), calls=%async_computation.1 | async-start | bytes 917504 | tf_op jit(solution)/shard_map/all_to_all | solution.py:91
  74.0 10.5 %copy-start.11 = (f32[16,2]{0,1:T(2,128)S(1)}, f32[16,2]{0,1:T(2,128)}, u32[]{:S(2)}) copy-start(f32[16,2]{0,1:T(2,128)} %param.14) | copy-start | bytes 388
  79.6 16.6 %all-to-all-start.3 = ((bf16[8,5,3584]{2,1,0:T(8,128)(2,1)}), bf16[8,5,3584]{2,1,0:T(8,128)(2,1)S(1)}, u32[]{:S(2)}, u32[]{:S(2)}) async-start(bf16[8,5,3584]{2,1,0:T(8,128)(2,1)} %reshape.125), calls=%async_computation.3 | async-start | bytes 917504 | tf_op jit(solution)/shard_map/all_to_all | solution.py:91
Sparse Core Ops, SparseCore 0:
  19.7 38.1 reduce-scatter.3
where the time goes:
time: 108 us; the launch traced here: 107 us
  waiting for transfers between devices  32.1 us (30%)
  local copies, waits for them, and re-layouts  24.5 us (23%)
  starting transfers between devices  18.7 us (17%)
  between operations  14.4 us (13%)
  matrix products  14.2 us (13%)
  other arithmetic  2.71 us (3%)
    all_to_all x2, waiting for transfers between devices, dispatch(): lax.all_to_all(outgoing, 'expert', split_axis=1, concat_axis=1, tiled=True)  17.3 us
    all_to_all x2, waiting for transfers between devices, dispatch(): lax.all_to_all(partial_value.reshape(experts_axis, slot_count, row_width)...  14.8 us
    all_to_all x2, starting transfers between devices, dispatch(): lax.all_to_all(outgoing, 'expert', split_axis=1, concat_axis=1, tiled=True)  10.9 us
    unnamed x32, local copies, waits for them, and re-layouts  8.84 us
    all_to_all x2, starting transfers between devices, dispatch(): lax.all_to_all(partial_value.reshape(experts_axis, slot_count, row_width)...  7.75 us
    slice x1, local copies, waits for them, and re-layouts, backward_work(): stacked[0]  3.44 us
    dot_general x3, matrix products, forward_factors(): jnp.dot(block_rows, slice_gate, preferred_element_type=jnp.float32)  3.2 us
    reshape x2, local copies, waits for them, and re-layouts, dispatch(): partial_value.reshape(experts_axis, slot_count, row_width)  2.76 us
  transfers between devices with their start and end apart: 5, of which 4 were waited for; matrix products, arithmetic and copies ran while one was open for 24% of the time, Pallas kernels for 0%

commit v1 on v0

v1 whole, which is shorter than its diff:
```python
import functools

import jax
import jax.numpy as jnp
from jax import lax
from jax.experimental import pallas as pl
from jax.experimental.pallas import tpu as pltpu
from jax.sharding import PartitionSpec as P

EXPERTS = 8
CAP = 5
BLOCK = 16
FOLD = 3
GROUP = 8
BF16 = jnp.bfloat16
F32 = jnp.float32
MESH = pl.DeviceIdType.MESH


def mm(a, b):
    return jnp.dot(a, b, preferred_element_type=F32)


def mm_nt(a, b):
    return lax.dot_general(a, b, (((1,), (1,)), ((), ())), preferred_element_type=F32)


def mm_tn(a, b):
    return lax.dot_general(a, b, (((0,), (0,)), ((), ())), preferred_element_type=F32)


def slots(routes, width, slices):
    count = routes.shape[0]
    lane = lax.broadcasted_iota(jnp.int32, (count, width), 1)
    expert = lane // (BLOCK * slices)
    at = lane % BLOCK
    first = routes[:, 0:1] == expert
    second = routes[:, 1:2] == expert
    named = jnp.where(first | second, 1.0, 0.0).astype(BF16)
    row = lax.broadcasted_iota(jnp.int32, (count, count), 0)
    column = lax.broadcasted_iota(jnp.int32, (count, count), 1)
    before = jnp.where(column < row, 1.0, 0.0).astype(BF16)
    position = mm(before, named)
    here = (position == (at % CAP).astype(F32)) & (at < FOLD * CAP)
    return first & here, second & here, at // CAP


def ones(mask):
    return jnp.where(mask, 1.0, 0.0).astype(BF16)


def kernel(
    n, ne, tok1, rt1, gt1, tok2, rt2, gt2, cot2, rows3, cot3, wg_hbm, wu_hbm, wd_hbm,
    out1, dx2, grads,
    wgu, wd, stack, snd, rcv, ret_snd, ret_rcv, snd3, rcv3, fac_snd, fac_rcv,
    w_sem, own_sem, snd_sem, rcv_sem, ret_snd_sem, ret_rcv_sem, e_snd_sem, e_rcv_sem,
):
    depth = tok1.shape[1]
    h = wd.shape[1]
    chunk = wd.shape[2]
    slices = n // EXPERTS
    span = depth // ne
    spans = [(j * chunk, min(chunk, depth - j * chunk)) for j in range(FOLD)]
    me = lax.axis_index("expert")
    mine = lax.axis_index("edata")

    def expert_peer(k):
        return lax.rem(me + k, n)

    def edata_peer(k):
        return lax.rem(mine + k, ne)

    barrier = pltpu.get_barrier_semaphore()
    for k in range(1, n):
        pl.semaphore_signal(barrier, inc=1, device_id=(mine, expert_peer(k)), device_id_type=MESH)
    for k in range(1, ne):
        pl.semaphore_signal(barrier, inc=1, device_id=(edata_peer(k), me), device_id_type=MESH)

    loads = []
    for j, (at, size) in enumerate(spans):
        loads.append(pltpu.make_async_copy(
            wg_hbm.at[pl.ds(at, size), :], wgu.at[j, pl.ds(0, size), pl.ds(0, h)], w_sem.at[len(loads)]))
        loads.append(pltpu.make_async_copy(
            wu_hbm.at[pl.ds(at, size), :], wgu.at[j, pl.ds(0, size), pl.ds(h, h)], w_sem.at[len(loads)]))
        loads.append(pltpu.make_async_copy(
            wd_hbm.at[:, pl.ds(at, size)], wd.at[j, :, pl.ds(0, size)], w_sem.at[len(loads)]))
    for load in loads:
        load.start()
    for j, (at, size) in enumerate(spans):
        if size < chunk:
            wgu[j, size:, :] = jnp.zeros((chunk - size, 2 * h), BF16)
            wd[j, :, size:] = jnp.zeros((h, chunk - size), BF16)
            for k in range(2):
                base = (k * FOLD + j) * BLOCK
                stack[base:base + BLOCK, size:] = jnp.zeros((BLOCK, chunk - size), BF16)

    def send_copy(u, k):
        peer = expert_peer(k)
        return pltpu.make_async_remote_copy(
            src_ref=snd.at[u, peer // slices], dst_ref=rcv.at[u, me],
            send_sem=snd_sem.at[u, k], recv_sem=rcv_sem.at[u, k],
            device_id=(mine, peer), device_id_type=MESH)

    def own_copy(u):
        return pltpu.make_async_copy(snd.at[u, me // slices], rcv.at[u, me], own_sem.at[u])

    def ret_copy(u, k):
        peer = expert_peer(k)
        return pltpu.make_async_remote_copy(
            src_ref=ret_snd.at[u, peer], dst_ref=ret_rcv.at[u, me],
            send_sem=ret_snd_sem.at[u, k], recv_sem=ret_rcv_sem.at[u, k],
            device_id=(mine, peer), device_id_type=MESH)

    def own_ret(u):
        return pltpu.make_async_copy(ret_snd.at[u, me], ret_rcv.at[u, me], own_sem.at[3 + u])

    def rows_copy(k):
        peer = edata_peer(k)
        return pltpu.make_async_remote_copy(
            src_ref=snd3.at[peer], dst_ref=rcv3.at[mine],
            send_sem=e_snd_sem.at[0, k], recv_sem=e_rcv_sem.at[0, k],
            device_id=(peer, me), device_id_type=MESH)

    def factor_copy(k):
        return pltpu.make_async_remote_copy(
            src_ref=fac_snd, dst_ref=fac_rcv.at[mine],
            send_sem=e_snd_sem.at[1, k], recv_sem=e_rcv_sem.at[1, k],
            device_id=(edata_peer(k), me), device_id_type=MESH)

    own_rows = pltpu.make_async_copy(snd3.at[mine], rcv3.at[mine], own_sem.at[5])
    own_factors = pltpu.make_async_copy(fac_snd, fac_rcv.at[mine], own_sem.at[6])

    def pack(u, masks, values, chunk_of):
        chosen = []
        for i, (mask, value) in enumerate(zip(masks, values)):
            for j, (at, size) in enumerate(spans):
                base = (i * FOLD + j) * BLOCK
                stack[base:base + BLOCK, 0:size] = value(at, size)
                chosen.append(ones(mask & (chunk_of == j)))
        picked = jnp.concatenate(chosen, axis=0)
        packed = mm_tn(picked, stack[0:picked.shape[0], :]).astype(BF16)
        snd[u] = packed.reshape(EXPERTS, BLOCK, chunk)

    width = EXPERTS * BLOCK
    first_one, second_one, chunk_of = slots(rt1[...], width, 1)
    pack(0, [first_one | second_one], [lambda at, size: tok1[:, at:at + size]], chunk_of)

    pl.semaphore_wait(barrier, n + ne - 2)
    order = list(range(1, n))
    for k in order:
        send_copy(0, k).start()
    own_copy(0).start()

    first_two, second_two, _ = slots(rt2[...], width, 1)
    pack(1, [first_two | second_two], [lambda at, size: tok2[:, at:at + size]], chunk_of)
    for k in order:
        send_copy(1, k).start()
    own_copy(1).start()

    def scaled(k):
        return lambda at, size: (gt2[:, k:k + 1] * cot2[:, at:at + size].astype(F32)).astype(BF16)

    pack(2, [first_two, second_two], [scaled(0), scaled(1)], chunk_of)
    for k in order:
        send_copy(2, k).start()
    own_copy(2).start()

    count3 = rows3.shape[0]
    for j in range(ne):
        snd3[j, 0:count3, :] = rows3[:, j * span:(j + 1) * span]
        snd3[j, count3:2 * count3, :] = cot3[:, j * span:(j + 1) * span]
    for k in range(1, ne):
        rows_copy(k).start()
    own_rows.start()

    for load in loads:
        load.wait()

    def activations(gate_up):
        gate = gate_up[:, 0:h]
        up = gate_up[:, h:2 * h]
        return gate, up, jax.nn.sigmoid(gate)

    def cotangents(d_hidden, gate, up, sigma):
        d_gate = (d_hidden * up * sigma * (1.0 + gate * (1.0 - sigma))).astype(BF16)
        d_up = (d_hidden * gate * sigma).astype(BF16)
        return d_gate, d_up

    gate_up = jnp.zeros((count3, 2 * h), F32)
    d_hidden = jnp.zeros((count3, h), F32)
    for j, (at, size) in enumerate(spans):
        gate_up = gate_up + mm(rows3[:, at:at + size], wgu[j, 0:size, :])
        d_hidden = d_hidden + mm_nt(cot3[:, at:at + size], wd[j, :, 0:size])
    gate, up, sigma = activations(gate_up)
    d_gate, d_up = cotangents(d_hidden, gate, up, sigma)
    fac_snd[:, 0:h] = d_gate
    fac_snd[:, h:2 * h] = d_up
    fac_snd[:, 2 * h:3 * h] = (gate * sigma * up).astype(BF16)
    for k in range(1, ne):
        factor_copy(k).start()
    own_factors.start()

    rows = GROUP * BLOCK
    row = lax.broadcasted_iota(jnp.int32, (rows, rows), 0)
    column = lax.broadcasted_iota(jnp.int32, (rows, rows), 1)
    join = jnp.where(
        (row // BLOCK == column // BLOCK)
        & (row % BLOCK % CAP == column % BLOCK % CAP)
        & (row % BLOCK < FOLD * CAP)
        & (column % BLOCK < FOLD * CAP),
        1.0, 0.0)

    def chunk_mask(j, size):
        slot = lax.broadcasted_iota(jnp.int32, (rows, size), 0) % BLOCK
        return slot // CAP == j

    def joined(parts):
        total = jnp.zeros_like(parts[0])
        for j, part in enumerate(parts):
            total = total + jnp.where(chunk_mask(j, part.shape[1]), part, 0.0)
        return jnp.dot(join, total, precision=lax.Precision.HIGHEST, preferred_element_type=F32)

    def spread(value, j):
        return jnp.where(chunk_mask(j, value.shape[1]), value, 0.0).astype(BF16)

    def groups(body):
        if n == GROUP:
            body(0)
        else:
            pl.loop(0, n // GROUP)(lambda b: body(b * GROUP))

    def block(ref, u, b):
        return ref[u, pl.ds(b, GROUP)].reshape(rows, chunk)

    def forward(b):
        x = block(rcv, 0, b)
        gate, up, sigma = activations(joined([mm(x, wgu[j]) for j in range(FOLD)]))
        hidden = gate * sigma * up
        total = sum(mm(spread(hidden, j), wd[j]) for j in range(FOLD))
        ret_snd[0, pl.ds(b, GROUP)] = total.astype(BF16).reshape(GROUP, BLOCK, chunk)

    def backward(b):
        x = block(rcv, 1, b)
        y = block(rcv, 2, b)
        gate, up, sigma = activations(joined([mm(x, wgu[j]) for j in range(FOLD)]))
        d_hidden = joined([mm_nt(y, wd[j]) for j in range(FOLD)])
        d_gate, d_up = cotangents(d_hidden, gate, up, sigma)
        both = jnp.concatenate([d_gate.astype(F32), d_up.astype(F32)], axis=1)
        total = sum(mm_nt(spread(both, j), wgu[j]) for j in range(FOLD))
        ret_snd[1, pl.ds(b, GROUP)] = total.astype(BF16).reshape(GROUP, BLOCK, chunk)

    for k in order:
        send_copy(0, k).wait_recv()
    own_copy(0).wait()
    groups(forward)
    for k in order:
        ret_copy(0, k).start()
    own_ret(0).start()

    for k in range(1, ne):
        rows_copy(k).wait_recv()
        factor_copy(k).wait_recv()
    own_rows.wait()
    own_factors.wait()
    all_rows = rcv3[:, 0:count3, :].reshape(ne * count3, span)
    all_cots = rcv3[:, count3:2 * count3, :].reshape(ne * count3, span)
    factors = fac_rcv[...].reshape(ne * count3, 3 * h)
    pair = mm_tn(all_rows, factors[:, 0:2 * h]).astype(BF16)
    grads[0] = pair[:, 0:h]
    grads[1] = pair[:, h:2 * h]
    grads[2] = mm_tn(all_cots, factors[:, 2 * h:3 * h]).astype(BF16)

    for u in (1, 2):
        for k in order:
            send_copy(u, k).wait_recv()
        own_copy(u).wait()
    groups(backward)
    for k in order:
        ret_copy(1, k).start()
    own_ret(1).start()

    back = n * BLOCK

    for k in order:
        ret_copy(0, k).wait_recv()
    own_ret(0).wait()
    first, second, back_chunk = slots(rt1[...], back, slices)
    weight = jnp.where(first, gt1[:, 0:1], 0.0) + jnp.where(second, gt1[:, 1:2], 0.0)
    high = weight.astype(BF16)
    rest = weight - high.astype(F32)
    middle = rest.astype(BF16)
    low = (rest - middle.astype(F32)).astype(BF16)
    answer = ret_rcv[0].reshape(back, chunk)
    for j, (at, size) in enumerate(spans):
        select = jnp.where(back_chunk == j, 1.0, 0.0)
        pieces = jnp.concatenate(
            [(piece.astype(F32) * select).astype(BF16) for piece in (high, middle, low)], axis=0)
        result = mm(pieces, answer[:, 0:size])
        out1[:, at:at + size] = (
            result[0:BLOCK] + result[BLOCK:2 * BLOCK] + result[2 * BLOCK:3 * BLOCK]).astype(BF16)

    for k in order:
        ret_copy(1, k).wait_recv()
    own_ret(1).wait()
    first, second, back_chunk = slots(rt2[...], back, slices)
    answer = ret_rcv[1].reshape(back, chunk)
    for j, (at, size) in enumerate(spans):
        picked = ones((first | second) & (back_chunk == j))
        dx2[:, at:at + size] = mm(picked, answer[:, 0:size]).astype(BF16)

    for k in order:
        for u in range(3):
            send_copy(u, k).wait_send()
        for u in range(2):
            ret_copy(u, k).wait_send()
    for k in range(1, ne):
        rows_copy(k).wait_send()
        factor_copy(k).wait_send()


def shards(*args):
    n = lax.axis_size("expert")
    ne = lax.axis_size("edata")
    tokens, depth = args[0].shape
    count3 = args[7].shape[0]
    h = args[9].shape[1]
    span = depth // ne
    chunk = -(-depth // (FOLD * 128)) * 128
    vmem = pl.BlockSpec(memory_space=pltpu.VMEM)
    hbm = pl.BlockSpec(memory_space=pl.ANY)
    out_one, dx_two, grads = pl.pallas_call(
        functools.partial(kernel, n, ne),
        out_shape=(
            jax.ShapeDtypeStruct((tokens, depth), BF16),
            jax.ShapeDtypeStruct((tokens, depth), BF16),
            jax.ShapeDtypeStruct((3, span, h), BF16),
        ),
        in_specs=[vmem] * 9 + [hbm] * 3,
        out_specs=(vmem, vmem, vmem),
        scratch_shapes=[
            pltpu.VMEM((FOLD, chunk, 2 * h), BF16),
            pltpu.VMEM((FOLD, h, chunk), BF16),
            pltpu.VMEM((2 * FOLD * BLOCK, chunk), BF16),
            pltpu.VMEM((3, EXPERTS, BLOCK, chunk), BF16),
            pltpu.VMEM((3, n, BLOCK, chunk), BF16),
            pltpu.VMEM((2, n, BLOCK, chunk), BF16),
            pltpu.VMEM((2, n, BLOCK, chunk), BF16),
            pltpu.VMEM((ne, 2 * count3, span), BF16),
            pltpu.VMEM((ne, 2 * count3, span), BF16),
            pltpu.VMEM((count3, 3 * h), BF16),
            pltpu.VMEM((ne, count3, 3 * h), BF16),
            pltpu.SemaphoreType.DMA((3 * FOLD,)),
            pltpu.SemaphoreType.DMA((7,)),
            pltpu.SemaphoreType.DMA((3, n)),
            pltpu.SemaphoreType.DMA((3, n)),
            pltpu.SemaphoreType.DMA((2, n)),
            pltpu.SemaphoreType.DMA((2, n)),
            pltpu.SemaphoreType.DMA((2, ne)),
            pltpu.SemaphoreType.DMA((2, ne)),
        ],
        compiler_params=pltpu.CompilerParams(
            collective_id=0, has_side_effects=True, vmem_limit_bytes=48 * 2**20),
    )(*args)
    return out_one, dx_two, jnp.transpose(grads, (1, 0, 2))


def solution(mesh):
    both = P(("edata", "expert"), None)
    return jax.shard_map(
        shards,
        mesh=mesh,
        in_specs=(both,) * 9 + (P(None, "expert"), P(None, "expert"), P("expert", None)),
        out_specs=(both, both, P("edata", None, "expert")),
        check_vma=False,
    )
```

time: 108 us -> 55.2 us (0.51)
  Pallas kernels: 0 us -> 41.7 us
  waiting for transfers between devices: 32.1 us -> 0 us
  starting transfers between devices: 18.7 us -> 0 us
  matrix products: 14.2 us -> 0 us
  between operations: 14.4 us -> 0.66 us
  local copies, waits for them, and re-layouts: 24.5 us -> 12.4 us
  other arithmetic: 2.71 us -> 0 us
    pallas_call x0 -> x1, Pallas kernels: none -> 41.7 us  [shards(): pl.pallas_call(functools.partial(kernel, n, ne), out_shape=(jax.ShapeDtyp...]
    all_to_all x4 -> x0, waiting for transfers between devices: 32.1 us -> none  [the longest x2 17.3 us: dispatch(): lax.all_to_all(outgoing, 'expert', split_axis=1, concat_axis=1, tiled=True)]
    all_to_all x4 -> x0, starting transfers between devices: 18.7 us -> none  [the longest x2 10.9 us: dispatch(): lax.all_to_all(outgoing, 'expert', split_axis=1, concat_axis=1, tiled=True)]
    dot_general x17 -> x0, matrix products: 14.2 us -> none  [the longest x3 3.2 us: forward_factors(): jnp.dot(block_rows, slice_gate, preferred_element_type=jnp.float32)]
    another operation x5 -> x0, local copies, waits for them, and re-layouts: 4.51 us -> none  [the longest x1 1.89 us: forward_work(): stacked[0]]
    reshape x8 -> x0, local copies, waits for them, and re-layouts: 4.38 us -> none  [the longest x2 2.76 us: dispatch(): partial_value.reshape(experts_axis, slot_count, row_width)]
    unnamed x32 -> x29, local copies, waits for them, and re-layouts: 8.84 us -> 12.4 us
    slice x1 -> x0, local copies, waits for them, and re-layouts: 3.44 us -> none  [backward_work(): stacked[0]]
  transfers between devices with their start and end apart: 5 -> 0, of which waited for: 4 -> 0; matrix products, arithmetic and copies ran while one was open for 24% -> 0% of each run, Pallas kernels for 0% -> 0%
where the time goes in v1:
time: 55.2 us; the launch traced here: 54.8 us
  Pallas kernels  41.7 us (76%)
  local copies, waits for them, and re-layouts  12.4 us (22%)
  between operations  0.66 us (1%)
    pallas_call x1, Pallas kernels, shards(): pl.pallas_call(functools.partial(kernel, n, ne), out_shape=(jax.ShapeDtyp...  41.7 us
    unnamed x29, local copies, waits for them, and re-layouts  12.4 us

profile of v1, /device:TPU:0, one launch (start us, length us, event | category | flops | bytes accessed | tf_op | source)
XLA Modules:
  0.0 54.8 jit_solution(14904064252770926692)
XLA Ops:
  0.6 0.0 copy-start.8
  0.6 0.8 %copy.15.rt1 = s32[16,2]{1,0:T(8,128)S(1)} copy(s32[16,2]{0,1:T(2,128)} %param.13) | data formatting | bytes 256 | tf_op args[1]
  1.4 0.0 copy-done.8
  1.4 0.0 copy-start.9
  1.4 0.1 copy.16.gt1
  1.5 0.6 %copy-done.9 = s32[16,2]{0,1:T(2,128)S(1)} copy-done((s32[16,2]{0,1:T(2,128)S(1)}, s32[16,2]{0,1:T(2,128)}, u32[]{:S(2)}) %copy-start.9) | copy-done | bytes 152
  2.1 0.0 copy-start.10
  2.1 0.1 copy.17.rt2
  2.2 0.6 %copy-done.10 = f32[16,2]{0,1:T(2,128)S(1)} copy-done((f32[16,2]{0,1:T(2,128)S(1)}, f32[16,2]{0,1:T(2,128)}, u32[]{:S(2)}) %copy-start.10) | copy-done | bytes 152
  2.8 0.1 copy.18.gt2
  2.8 0.0 copy-start
  2.8 1.2 %copy-done = bf16[3584,128]{1,0:T(8,128)(2,1)S(1)} copy-done((bf16[3584,128]{1,0:T(8,128)(2,1)S(1)}, bf16[3584,128]{1,0:T(8,128)(2,1)}, u32[]{:S(2)}) %copy-start) | copy-done | bytes 917528
  4.0 0.0 copy-start.1
  4.0 1.2 %copy-done.1 = bf16[3584,128]{1,0:T(8,128)(2,1)S(1)} copy-done((bf16[3584,128]{1,0:T(8,128)(2,1)S(1)}, bf16[3584,128]{1,0:T(8,128)(2,1)}, u32[]{:S(2)}) %copy-start.1) | copy-done | bytes 917528
  5.2 0.0 copy-start.2
  5.2 1.2 %copy-done.2 = bf16[128,3584]{1,0:T(8,128)(2,1)S(1)} copy-done((bf16[128,3584]{1,0:T(8,128)(2,1)S(1)}, bf16[128,3584]{1,0:T(8,128)(2,1)}, u32[]{:S(2)}) %copy-start.2) | copy-done | bytes 917528
  6.4 0.0 copy-start.3
  6.4 0.9 %copy-done.3 = bf16[32,3584]{1,0:T(8,128)(2,1)S(1)} copy-done((bf16[32,3584]{1,0:T(8,128)(2,1)S(1)}, bf16[32,3584]{1,0:T(8,128)(2,1)}, u32[]{:S(2)}) %copy-start.3) | copy-done | bytes 229400
  7.3 0.0 copy-start.4
  7.3 0.9 %copy-done.4 = bf16[32,3584]{1,0:T(8,128)(2,1)S(1)} copy-done((bf16[32,3584]{1,0:T(8,128)(2,1)S(1)}, bf16[32,3584]{1,0:T(8,128)(2,1)}, u32[]{:S(2)}) %copy-start.4) | copy-done | bytes 229400
  8.3 0.0 copy-start.5
  8.3 0.9 %copy-done.5 = bf16[16,3584]{1,0:T(8,128)(2,1)S(1)} copy-done((bf16[16,3584]{1,0:T(8,128)(2,1)S(1)}, bf16[16,3584]{1,0:T(8,128)(2,1)}, u32[]{:S(2)}) %copy-start.5) | copy-done | bytes 114712
  9.2 0.0 copy-start.6
  9.2 0.9 %copy-done.6 = bf16[16,3584]{1,0:T(8,128)(2,1)S(1)} copy-done((bf16[16,3584]{1,0:T(8,128)(2,1)S(1)}, bf16[16,3584]{1,0:T(8,128)(2,1)}, u32[]{:S(2)}) %copy-start.6) | copy-done | bytes 114712
  10.1 0.0 copy-start.7
  10.1 0.9 %copy-done.7 = bf16[16,3584]{1,0:T(8,128)(2,1)S(1)} copy-done((bf16[16,3584]{1,0:T(8,128)(2,1)S(1)}, bf16[16,3584]{1,0:T(8,128)(2,1)}, u32[]{:S(2)}) %copy-start.7) | copy-done | bytes 114712
  11.0 41.7 %shard_map.139 = (bf16[16,3584]{1,0:T(8,128)(2,1)S(1)}, bf16[16,3584]{1,0:T(8,128)(2,1)S(1)}, bf16[3,896,128]{2,1,0:T(8,128)(2,1)S(1)}) custom-call(bf16[16,3584]{1,0:T(8,128)(2,1)S(1)} %copy-done.5, s32[16,2]{1,0:T(8,128)S(1)} %copy.15.rt1, f32[16,2]{1,0:T(8,128)S(1)} %copy.16.gt1, bf16[16,3584]{1,0:T(8,128)(2,1)S(1)} %copy-done.6, s32[16,2]{1,0:T(8,128)S(1)} %copy.17.rt2, ...), custom_call_target="tpu_custom_call" | custom-call | tf_op jit(solution)/shard_map/pallas_call | solution.py:331
  52.6 0.6 %copy.22 = bf16[16,3584]{1,0:T(8,128)(2,1)} copy(bf16[16,3584]{1,0:T(8,128)(2,1)S(1)} %get-tuple-element.12) | data formatting | bytes 229376
  53.3 0.6 %copy.23 = bf16[16,3584]{1,0:T(8,128)(2,1)} copy(bf16[16,3584]{1,0:T(8,128)(2,1)S(1)} %get-tuple-element.13) | data formatting | bytes 229376
  53.9 0.8 %copy.24 = bf16[896,3,128]{2,0,1:T(8,128)(2,1)} copy(bf16[896,3,128]{2,0,1:T(8,128)(2,1)S(1)} %bitcast.1) | data formatting | bytes 1376256
Async XLA Ops:
  0.6 0.8 %copy-start.8 = (f32[16,2]{0,1:T(2,128)S(1)}, f32[16,2]{0,1:T(2,128)}, u32[]{:S(2)}) copy-start(f32[16,2]{0,1:T(2,128)} %param.14) | copy-start | bytes 388
  1.4 0.7 %copy-start.9 = (s32[16,2]{0,1:T(2,128)S(1)}, s32[16,2]{0,1:T(2,128)}, u32[]{:S(2)}) copy-start(s32[16,2]{0,1:T(2,128)} %param.16) | copy-start | bytes 388
  2.1 0.7 %copy-start.10 = (f32[16,2]{0,1:T(2,128)S(1)}, f32[16,2]{0,1:T(2,128)}, u32[]{:S(2)}) copy-start(f32[16,2]{0,1:T(2,128)} %param.17) | copy-start | bytes 388
  2.8 1.2 %copy-start = (bf16[3584,128]{1,0:T(8,128)(2,1)S(1)}, bf16[3584,128]{1,0:T(8,128)(2,1)}, u32[]{:S(2)}) copy-start(bf16[3584,128]{1,0:T(8,128)(2,1)} %wg_hbm.1) | copy-start | bytes 2752516
  4.0 1.2 %copy-start.1 = (bf16[3584,128]{1,0:T(8,128)(2,1)S(1)}, bf16[3584,128]{1,0:T(8,128)(2,1)}, u32[]{:S(2)}) copy-start(bf16[3584,128]{1,0:T(8,128)(2,1)} %wu_hbm.1) | copy-start | bytes 2752516
  5.2 1.2 %copy-start.2 = (bf16[128,3584]{1,0:T(8,128)(2,1)S(1)}, bf16[128,3584]{1,0:T(8,128)(2,1)}, u32[]{:S(2)}) copy-start(bf16[128,3584]{1,0:T(8,128)(2,1)} %wd_hbm.1) | copy-start | bytes 2752516
  6.4 0.9 %copy-start.3 = (bf16[32,3584]{1,0:T(8,128)(2,1)S(1)}, bf16[32,3584]{1,0:T(8,128)(2,1)}, u32[]{:S(2)}) copy-start(bf16[32,3584]{1,0:T(8,128)(2,1)} %rows3.1) | copy-start | bytes 688132
  7.3 0.9 %copy-start.4 = (bf16[32,3584]{1,0:T(8,128)(2,1)S(1)}, bf16[32,3584]{1,0:T(8,128)(2,1)}, u32[]{:S(2)}) copy-start(bf16[32,3584]{1,0:T(8,128)(2,1)} %cot3.1) | copy-start | bytes 688132
  8.3 0.9 %copy-start.5 = (bf16[16,3584]{1,0:T(8,128)(2,1)S(1)}, bf16[16,3584]{1,0:T(8,128)(2,1)}, u32[]{:S(2)}) copy-start(bf16[16,3584]{1,0:T(8,128)(2,1)} %tok1.1) | copy-start | bytes 344068
  9.2 0.9 %copy-start.6 = (bf16[16,3584]{1,0:T(8,128)(2,1)S(1)}, bf16[16,3584]{1,0:T(8,128)(2,1)}, u32[]{:S(2)}) copy-start(bf16[16,3584]{1,0:T(8,128)(2,1)} %tok2.1) | copy-start | bytes 344068
  10.1 0.9 %copy-start.7 = (bf16[16,3584]{1,0:T(8,128)(2,1)S(1)}, bf16[16,3584]{1,0:T(8,128)(2,1)}, u32[]{:S(2)}) copy-start(bf16[16,3584]{1,0:T(8,128)(2,1)} %cot2.1) | copy-start | bytes 344068

commit v2 on v1

--- a/solution.py
+++ b/solution.py
@@ -30,19 +30,26 @@
 
 
 def slots(routes, width, slices):
-    count = routes.shape[0]
-    lane = lax.broadcasted_iota(jnp.int32, (count, width), 1)
-    expert = lane // (BLOCK * slices)
-    at = lane % BLOCK
-    first = routes[:, 0:1] == expert
-    second = routes[:, 1:2] == expert
+    count = routes.shape[1]
+    row = lax.broadcasted_iota(jnp.int32, (width, count), 0)
+    expert = row // (BLOCK * slices)
+    at = row % BLOCK
+    first = routes[0:1, :] == expert
+    second = routes[1:2, :] == expert
     named = jnp.where(first | second, 1.0, 0.0).astype(BF16)
+    earlier = lax.broadcasted_iota(jnp.int32, (count, count), 0)
+    later = lax.broadcasted_iota(jnp.int32, (count, count), 1)
+    before = jnp.where(earlier < later, 1.0, 0.0).astype(BF16)
+    position = mm(named, before)
+    here = (position == (at % CAP).astype(F32)) & (at < FOLD * CAP)
+    return first & here, second & here, at // CAP
+
+
+def turned(piece):
+    count = piece.shape[1]
     row = lax.broadcasted_iota(jnp.int32, (count, count), 0)
     column = lax.broadcasted_iota(jnp.int32, (count, count), 1)
-    before = jnp.where(column < row, 1.0, 0.0).astype(BF16)
-    position = mm(before, named)
-    here = (position == (at % CAP).astype(F32)) & (at < FOLD * CAP)
-    return first & here, second & here, at // CAP
+    return mm_nt(jnp.where(row == column, 1.0, 0.0).astype(BF16), piece).astype(BF16)
 
 
 def ones(mask):
@@ -50,8 +57,10 @@
 
 
 def kernel(
-    n, ne, tok1, rt1, gt1, tok2, rt2, gt2, cot2, rows3, cot3, wg_hbm, wu_hbm, wd_hbm,
+    n, ne, tok1_hbm, rt1_hbm, gt1_hbm, tok2_hbm, rt2_hbm, gt2_hbm, cot2_hbm, rows3_hbm, cot3_hbm,
+    wg_hbm, wu_hbm, wd_hbm,
     out1, dx2, grads,
+    tok1, rt1, gt1, tok2, rt2, gt2, cot2, rows3, cot3, in_sem,
     wgu, wd, stack, snd, rcv, ret_snd, ret_rcv, snd3, rcv3, fac_snd, fac_rcv,
     w_sem, own_sem, snd_sem, rcv_sem, ret_snd_sem, ret_rcv_sem, e_snd_sem, e_rcv_sem,
 ):
@@ -76,6 +85,12 @@
     for k in range(1, ne):
         pl.semaphore_signal(barrier, inc=1, device_id=(edata_peer(k), me), device_id_type=MESH)
 
+    pairs = (
+        (rt1_hbm, rt1), (tok1_hbm, tok1), (rt2_hbm, rt2), (tok2_hbm, tok2), (gt2_hbm, gt2),
+        (cot2_hbm, cot2), (gt1_hbm, gt1), (rows3_hbm, rows3), (cot3_hbm, cot3))
+    inputs = [pltpu.make_async_copy(a, b, in_sem.at[i]) for i, (a, b) in enumerate(pairs)]
+    for load in inputs:
+        load.start()
     loads = []
     for j, (at, size) in enumerate(spans):
         loads.append(pltpu.make_async_copy(
@@ -90,9 +105,7 @@
         if size < chunk:
             wgu[j, size:, :] = jnp.zeros((chunk - size, 2 * h), BF16)
             wd[j, :, size:] = jnp.zeros((h, chunk - size), BF16)
-            for k in range(2):
-                base = (k * FOLD + j) * BLOCK
-                stack[base:base + BLOCK, size:] = jnp.zeros((BLOCK, chunk - size), BF16)
+            stack[j * BLOCK:(j + 1) * BLOCK, size:] = jnp.zeros((BLOCK, chunk - size), BF16)
 
     def send_copy(u, k):
         peer = expert_peer(k)
@@ -130,20 +143,21 @@
     own_rows = pltpu.make_async_copy(snd3.at[mine], rcv3.at[mine], own_sem.at[5])
     own_factors = pltpu.make_async_copy(fac_snd, fac_rcv.at[mine], own_sem.at[6])
 
-    def pack(u, masks, values, chunk_of):
-        chosen = []
-        for i, (mask, value) in enumerate(zip(masks, values)):
-            for j, (at, size) in enumerate(spans):
-                base = (i * FOLD + j) * BLOCK
-                stack[base:base + BLOCK, 0:size] = value(at, size)
-                chosen.append(ones(mask & (chunk_of == j)))
-        picked = jnp.concatenate(chosen, axis=0)
-        packed = mm_tn(picked, stack[0:picked.shape[0], :]).astype(BF16)
-        snd[u] = packed.reshape(EXPERTS, BLOCK, chunk)
+    def pack(u, mask, source, scale):
+        for j, (at, size) in enumerate(spans):
+            stack[j * BLOCK:(j + 1) * BLOCK, 0:size] = source[:, at:at + size]
+        total = jnp.zeros((width, chunk), F32)
+        for j in range(FOLD):
+            total = total + mm(ones(mask & (chunk_of == j)), stack[j * BLOCK:(j + 1) * BLOCK, :])
+        if scale is not None:
+            total = total * scale
+        snd[u] = total.astype(BF16).reshape(EXPERTS, BLOCK, chunk)
 
     width = EXPERTS * BLOCK
+    inputs[0].wait()
     first_one, second_one, chunk_of = slots(rt1[...], width, 1)
-    pack(0, [first_one | second_one], [lambda at, size: tok1[:, at:at + size]], chunk_of)
+    inputs[1].wait()
+    pack(0, first_one | second_one, tok1, None)
 
     pl.semaphore_wait(barrier, n + ne - 2)
     order = list(range(1, n))
@@ -151,16 +165,18 @@
         send_copy(0, k).start()
     own_copy(0).start()
 
+    for load in inputs[2:]:
+        load.wait()
     first_two, second_two, _ = slots(rt2[...], width, 1)
-    pack(1, [first_two | second_two], [lambda at, size: tok2[:, at:at + size]], chunk_of)
+    pack(1, first_two | second_two, tok2, None)
     for k in order:
         send_copy(1, k).start()
     own_copy(1).start()
 
-    def scaled(k):
-        return lambda at, size: (gt2[:, k:k + 1] * cot2[:, at:at + size].astype(F32)).astype(BF16)
-
-    pack(2, [first_two, second_two], [scaled(0), scaled(1)], chunk_of)
+    scale = (
+        jnp.where(first_two, gt2[0:1, :], 0.0) + jnp.where(second_two, gt2[1:2, :], 0.0)
+    ).sum(axis=1, keepdims=True)
+    pack(2, first_two | second_two, cot2, scale)
     for k in order:
         send_copy(2, k).start()
     own_copy(2).start()
@@ -280,33 +296,34 @@
     own_ret(1).start()
 
     back = n * BLOCK
+    first, second, back_chunk = slots(rt1[...], back, slices)
+    weight = jnp.where(first, gt1[0:1, :], 0.0) + jnp.where(second, gt1[1:2, :], 0.0)
+    pieces = []
+    for j in range(FOLD):
+        rest = jnp.where(back_chunk == j, weight, 0.0)
+        split = []
+        for _ in range(3):
+            split.append(rest.astype(BF16))
+            rest = rest - split[-1].astype(F32)
+        pieces.append(jnp.concatenate([turned(piece) for piece in split], axis=0))
+    first, second, back_chunk = slots(rt2[...], back, slices)
+    picked = [turned(ones((first | second) & (back_chunk == j))) for j in range(FOLD)]
 
     for k in order:
         ret_copy(0, k).wait_recv()
     own_ret(0).wait()
-    first, second, back_chunk = slots(rt1[...], back, slices)
-    weight = jnp.where(first, gt1[:, 0:1], 0.0) + jnp.where(second, gt1[:, 1:2], 0.0)
-    high = weight.astype(BF16)
-    rest = weight - high.astype(F32)
-    middle = rest.astype(BF16)
-    low = (rest - middle.astype(F32)).astype(BF16)
     answer = ret_rcv[0].reshape(back, chunk)
     for j, (at, size) in enumerate(spans):
-        select = jnp.where(back_chunk == j, 1.0, 0.0)
-        pieces = jnp.concatenate(
-            [(piece.astype(F32) * select).astype(BF16) for piece in (high, middle, low)], axis=0)
-        result = mm(pieces, answer[:, 0:size])
+        result = mm(pieces[j], answer[:, 0:size])
         out1[:, at:at + size] = (
             result[0:BLOCK] + result[BLOCK:2 * BLOCK] + result[2 * BLOCK:3 * BLOCK]).astype(BF16)
 
     for k in order:
         ret_copy(1, k).wait_recv()
     own_ret(1).wait()
-    first, second, back_chunk = slots(rt2[...], back, slices)
     answer = ret_rcv[1].reshape(back, chunk)
     for j, (at, size) in enumerate(spans):
-        picked = ones((first | second) & (back_chunk == j))
-        dx2[:, at:at + size] = mm(picked, answer[:, 0:size]).astype(BF16)
+        dx2[:, at:at + size] = mm(picked[j], answer[:, 0:size]).astype(BF16)
 
     for k in order:
         for u in range(3):
@@ -318,7 +335,18 @@
         factor_copy(k).wait_send()
 
 
+def store(a, b, c, a_out, b_out, c_out, sem):
+    copies = [
+        pltpu.make_async_copy(source, target, sem.at[i])
+        for i, (source, target) in enumerate(((a, a_out), (b, b_out), (c, c_out)))]
+    for copy in copies:
+        copy.start()
+    for copy in copies:
+        copy.wait()
+
+
 def shards(*args):
+    args = [arg.T if i in (1, 2, 4, 5) else arg for i, arg in enumerate(args)]
     n = lax.axis_size("expert")
     ne = lax.axis_size("edata")
     tokens, depth = args[0].shape
@@ -328,19 +356,21 @@
     chunk = -(-depth // (FOLD * 128)) * 128
     vmem = pl.BlockSpec(memory_space=pltpu.VMEM)
     hbm = pl.BlockSpec(memory_space=pl.ANY)
-    out_one, dx_two, grads = pl.pallas_call(
-        functools.partial(kernel, n, ne),
-        out_shape=(
+    results = (
             jax.ShapeDtypeStruct((tokens, depth), BF16),
             jax.ShapeDtypeStruct((tokens, depth), BF16),
             jax.ShapeDtypeStruct((3, span, h), BF16),
-        ),
-        in_specs=[vmem] * 9 + [hbm] * 3,
+    )
+    landed = pl.pallas_call(
+        functools.partial(kernel, n, ne),
+        out_shape=results,
+        in_specs=[hbm] * 12,
         out_specs=(vmem, vmem, vmem),
-        scratch_shapes=[
+        scratch_shapes=[pltpu.VMEM(arg.shape, arg.dtype) for arg in args[:9]] + [
+            pltpu.SemaphoreType.DMA((9,)),
             pltpu.VMEM((FOLD, chunk, 2 * h), BF16),
             pltpu.VMEM((FOLD, h, chunk), BF16),
-            pltpu.VMEM((2 * FOLD * BLOCK, chunk), BF16),
+            pltpu.VMEM((FOLD * BLOCK, chunk), BF16),
             pltpu.VMEM((3, EXPERTS, BLOCK, chunk), BF16),
             pltpu.VMEM((3, n, BLOCK, chunk), BF16),
             pltpu.VMEM((2, n, BLOCK, chunk), BF16),
@@ -359,8 +389,15 @@
             pltpu.SemaphoreType.DMA((2, ne)),
         ],
         compiler_params=pltpu.CompilerParams(
-            collective_id=0, has_side_effects=True, vmem_limit_bytes=48 * 2**20),
+            collective_id=0, has_side_effects=True, vmem_limit_bytes=62 * 2**20),
     )(*args)
+    out_one, dx_two, grads = pl.pallas_call(
+        store,
+        out_shape=results,
+        in_specs=[vmem] * 3,
+        out_specs=(hbm,) * 3,
+        scratch_shapes=[pltpu.SemaphoreType.DMA((3,))],
+    )(*landed)
     return out_one, dx_two, jnp.transpose(grads, (1, 0, 2))
 
 

time: 55.2 us -> 45.6 us (0.83)
  local copies, waits for them, and re-layouts: 12.4 us -> 0 us
  Pallas kernels: 41.7 us -> 44.8 us
    unnamed x29 -> x0, local copies, waits for them, and re-layouts: 12.4 us -> none
    pallas_call x1 -> x2, Pallas kernels: 41.7 us -> 44.8 us  [the longest x1 42.6 us: shards(): pl.pallas_call(functools.partial(kernel, n, ne), out_shape=results, in_sp...]
where the time goes in v2:
time: 45.6 us; the launch traced here: 45.4 us
  Pallas kernels  44.8 us (98%)
  between operations  0.64 us (1%)
    pallas_call x1, Pallas kernels, shards(): pl.pallas_call(functools.partial(kernel, n, ne), out_shape=results, in_sp...  42.6 us
    pallas_call x1, Pallas kernels, shards(): pl.pallas_call(store, out_shape=results, in_specs=[vmem] * 3, out_specs=(...  2.17 us

profile of v2, /device:TPU:0, one launch (start us, length us, event | category | flops | bytes accessed | tf_op | source)
XLA Modules:
  0.0 45.4 jit_solution(14558588225897220082)
XLA Ops:
  0.6 42.6 %shard_map.139 = (bf16[16,3584]{1,0:T(8,128)(2,1)}, bf16[16,3584]{1,0:T(8,128)(2,1)}, bf16[3,896,128]{2,1,0:T(8,128)(2,1)}) custom-call(bf16[16,3584]{1,0:T(8,128)(2,1)} %tok1_hbm.1, s32[2,16]{1,0:T(2,128)} %bitcast.5, f32[2,16]{1,0:T(2,128)} %bitcast.6, bf16[16,3584]{1,0:T(8,128)(2,1)} %tok2_hbm.1, s32[2,16]{1,0:T(2,128)} %bitcast.7, f32[2,16]{1,0:T(2,128)} %bitcast.8, ...), custom_call_target="tpu_custom_call" | custom-call | tf_op jit(solution)/shard_map/pallas_call | solution.py:364
  43.2 2.2 %shard_map.140 = (bf16[16,3584]{1,0:T(8,128)(2,1)}, bf16[16,3584]{1,0:T(8,128)(2,1)}, bf16[3,896,128]{2,1,0:T(8,128)(2,1)}) custom-call(bf16[16,3584]{1,0:T(8,128)(2,1)} %get-tuple-element.9.a, bf16[16,3584]{1,0:T(8,128)(2,1)} %get-tuple-element.10.b, bf16[3,896,128]{2,1,0:T(8,128)(2,1)} %get-tuple-element.11.c), custom_call_target="tpu_custom_call" | custom-call | tf_op jit(solution)/shard_map/pallas_call | solution.py:394

commit v3 on v2

--- a/solution.py
+++ b/solution.py
@@ -41,8 +41,10 @@
     later = lax.broadcasted_iota(jnp.int32, (count, count), 1)
     before = jnp.where(earlier < later, 1.0, 0.0).astype(BF16)
     position = mm(named, before)
-    here = (position == (at % CAP).astype(F32)) & (at < FOLD * CAP)
-    return first & here, second & here, at // CAP
+    here = position == (at % CAP).astype(F32)
+    pieces = [here & (at // CAP == j) for j in range(FOLD)]
+    pieces += [(position == float(c)) & (at == FOLD * CAP) for c in range(CAP)]
+    return first, second, pieces
 
 
 def turned(piece):
@@ -61,7 +63,8 @@
     wg_hbm, wu_hbm, wd_hbm,
     out1, dx2, grads,
     tok1, rt1, gt1, tok2, rt2, gt2, cot2, rows3, cot3, in_sem,
-    wgu, wd, stack, snd, rcv, ret_snd, ret_rcv, snd3, rcv3, fac_snd, fac_rcv,
+    out1_buf, dx2_buf, grads_buf, out_sem, wgu_tail, wd_tail,
+    wgu, wd, snd, rcv, ret_snd, ret_rcv, snd3, rcv3, fac_snd, fac_rcv,
     w_sem, own_sem, snd_sem, rcv_sem, ret_snd_sem, ret_rcv_sem, e_snd_sem, e_rcv_sem,
 ):
     depth = tok1.shape[1]
@@ -69,7 +72,9 @@
     chunk = wd.shape[2]
     slices = n // EXPERTS
     span = depth // ne
-    spans = [(j * chunk, min(chunk, depth - j * chunk)) for j in range(FOLD)]
+    spans = [(j * chunk, chunk) for j in range(FOLD)]
+    cut = FOLD * chunk
+    tail = depth - cut
     me = lax.axis_index("expert")
     mine = lax.axis_index("edata")
 
@@ -99,14 +104,14 @@
             wu_hbm.at[pl.ds(at, size), :], wgu.at[j, pl.ds(0, size), pl.ds(h, h)], w_sem.at[len(loads)]))
         loads.append(pltpu.make_async_copy(
             wd_hbm.at[:, pl.ds(at, size)], wd.at[j, :, pl.ds(0, size)], w_sem.at[len(loads)]))
+    for source, target in (
+        (wg_hbm.at[pl.ds(cut, tail), :], wgu_tail.at[:, pl.ds(0, h)]),
+        (wu_hbm.at[pl.ds(cut, tail), :], wgu_tail.at[:, pl.ds(h, h)]),
+        (wd_hbm.at[:, pl.ds(cut, tail)], wd_tail),
+    ):
+        loads.append(pltpu.make_async_copy(source, target, w_sem.at[len(loads)]))
     for load in loads:
         load.start()
-    for j, (at, size) in enumerate(spans):
-        if size < chunk:
-            wgu[j, size:, :] = jnp.zeros((chunk - size, 2 * h), BF16)
-            wd[j, :, size:] = jnp.zeros((h, chunk - size), BF16)
-            stack[j * BLOCK:(j + 1) * BLOCK, size:] = jnp.zeros((BLOCK, chunk - size), BF16)
-
     def send_copy(u, k):
         peer = expert_peer(k)
         return pltpu.make_async_remote_copy(
@@ -143,21 +148,28 @@
     own_rows = pltpu.make_async_copy(snd3.at[mine], rcv3.at[mine], own_sem.at[5])
     own_factors = pltpu.make_async_copy(fac_snd, fac_rcv.at[mine], own_sem.at[6])
 
-    def pack(u, mask, source, scale):
+    def with_tails(total, tails):
+        spare = chunk - CAP * tail
+        if spare:
+            tails = tails + [jnp.zeros((total.shape[0], spare), F32)]
+        return total + jnp.concatenate(tails, axis=1)
+
+    def pack(u, mask, pieces, source, scale):
+        picked = [ones(mask & piece) for piece in pieces]
+        total = jnp.zeros((width, chunk), F32)
         for j, (at, size) in enumerate(spans):
-            stack[j * BLOCK:(j + 1) * BLOCK, 0:size] = source[:, at:at + size]
-        total = jnp.zeros((width, chunk), F32)
-        for j in range(FOLD):
-            total = total + mm(ones(mask & (chunk_of == j)), stack[j * BLOCK:(j + 1) * BLOCK, :])
+            total = total + mm(picked[j], source[:, at:at + size])
+        tails = [mm(picked[FOLD + c], source[:, cut:]) for c in range(CAP)]
         if scale is not None:
-            total = total * scale
-        snd[u] = total.astype(BF16).reshape(EXPERTS, BLOCK, chunk)
+            total = total * scale(pieces[0] | pieces[1] | pieces[2])
+            tails = [part * scale(pieces[FOLD + c]) for c, part in enumerate(tails)]
+        snd[u] = with_tails(total, tails).astype(BF16).reshape(EXPERTS, BLOCK, chunk)
 
     width = EXPERTS * BLOCK
     inputs[0].wait()
-    first_one, second_one, chunk_of = slots(rt1[...], width, 1)
+    first_one, second_one, pieces_one = slots(rt1[...], width, 1)
     inputs[1].wait()
-    pack(0, first_one | second_one, tok1, None)
+    pack(0, first_one | second_one, pieces_one, tok1, None)
 
     pl.semaphore_wait(barrier, n + ne - 2)
     order = list(range(1, n))
@@ -167,16 +179,15 @@
 
     for load in inputs[2:]:
         load.wait()
-    first_two, second_two, _ = slots(rt2[...], width, 1)
-    pack(1, first_two | second_two, tok2, None)
+    first_two, second_two, pieces_two = slots(rt2[...], width, 1)
+    pack(1, first_two | second_two, pieces_two, tok2, None)
     for k in order:
         send_copy(1, k).start()
     own_copy(1).start()
 
-    scale = (
-        jnp.where(first_two, gt2[0:1, :], 0.0) + jnp.where(second_two, gt2[1:2, :], 0.0)
-    ).sum(axis=1, keepdims=True)
-    pack(2, first_two | second_two, cot2, scale)
+    gates = jnp.where(first_two, gt2[0:1, :], 0.0) + jnp.where(second_two, gt2[1:2, :], 0.0)
+    pack(2, first_two | second_two, pieces_two, cot2,
+         lambda mask: jnp.where(mask, gates, 0.0).sum(axis=1, keepdims=True))
     for k in order:
         send_copy(2, k).start()
     own_copy(2).start()
@@ -207,6 +218,8 @@
     for j, (at, size) in enumerate(spans):
         gate_up = gate_up + mm(rows3[:, at:at + size], wgu[j, 0:size, :])
         d_hidden = d_hidden + mm_nt(cot3[:, at:at + size], wd[j, :, 0:size])
+    gate_up = gate_up + mm(rows3[:, cut:], wgu_tail[...])
+    d_hidden = d_hidden + mm_nt(cot3[:, cut:], wd_tail[...])
     gate, up, sigma = activations(gate_up)
     d_gate, d_up = cotangents(d_hidden, gate, up, sigma)
     fac_snd[:, 0:h] = d_gate
@@ -219,21 +232,24 @@
     rows = GROUP * BLOCK
     row = lax.broadcasted_iota(jnp.int32, (rows, rows), 0)
     column = lax.broadcasted_iota(jnp.int32, (rows, rows), 1)
-    join = jnp.where(
-        (row // BLOCK == column // BLOCK)
-        & (row % BLOCK % CAP == column % BLOCK % CAP)
-        & (row % BLOCK < FOLD * CAP)
-        & (column % BLOCK < FOLD * CAP),
-        1.0, 0.0)
+    same = row // BLOCK == column // BLOCK
+    to, of = row % BLOCK, column % BLOCK
+    slot_row = same & (to < FOLD * CAP)
+    from_tail = slot_row & (of == FOLD * CAP)
+    join = jnp.concatenate(
+        [jnp.where(slot_row & (of < FOLD * CAP) & (to % CAP == of % CAP), 1.0, 0.0)]
+        + [jnp.where(from_tail & (to % CAP == c), 1.0, 0.0) for c in range(CAP)], axis=1)
+    to_tail = [ones(same & (to == FOLD * CAP) & (of == c)) for c in range(CAP)]
 
     def chunk_mask(j, size):
         slot = lax.broadcasted_iota(jnp.int32, (rows, size), 0) % BLOCK
         return slot // CAP == j
 
-    def joined(parts):
+    def joined(parts, tails):
         total = jnp.zeros_like(parts[0])
         for j, part in enumerate(parts):
             total = total + jnp.where(chunk_mask(j, part.shape[1]), part, 0.0)
+        total = jnp.concatenate([total] + tails, axis=0)
         return jnp.dot(join, total, precision=lax.Precision.HIGHEST, preferred_element_type=F32)
 
     def spread(value, j):
@@ -248,22 +264,32 @@
     def block(ref, u, b):
         return ref[u, pl.ds(b, GROUP)].reshape(rows, chunk)
 
+    def tails_of(x):
+        return [x[:, c * tail:(c + 1) * tail] for c in range(CAP)]
+
+    def gate_ups(x):
+        return joined(
+            [mm(x, wgu[j]) for j in range(FOLD)], [mm(part, wgu_tail[...]) for part in tails_of(x)])
+
+    def answer_with(total, last):
+        last = last.astype(BF16)
+        whole = with_tails(total, [mm(place, last) for place in to_tail])
+        return whole.astype(BF16).reshape(GROUP, BLOCK, chunk)
+
     def forward(b):
-        x = block(rcv, 0, b)
-        gate, up, sigma = activations(joined([mm(x, wgu[j]) for j in range(FOLD)]))
+        gate, up, sigma = activations(gate_ups(block(rcv, 0, b)))
         hidden = gate * sigma * up
         total = sum(mm(spread(hidden, j), wd[j]) for j in range(FOLD))
-        ret_snd[0, pl.ds(b, GROUP)] = total.astype(BF16).reshape(GROUP, BLOCK, chunk)
+        ret_snd[0, pl.ds(b, GROUP)] = answer_with(total, mm(hidden.astype(BF16), wd_tail[...]))
 
     def backward(b):
-        x = block(rcv, 1, b)
         y = block(rcv, 2, b)
-        gate, up, sigma = activations(joined([mm(x, wgu[j]) for j in range(FOLD)]))
-        d_hidden = joined([mm_nt(y, wd[j]) for j in range(FOLD)])
-        d_gate, d_up = cotangents(d_hidden, gate, up, sigma)
-        both = jnp.concatenate([d_gate.astype(F32), d_up.astype(F32)], axis=1)
-        total = sum(mm_nt(spread(both, j), wgu[j]) for j in range(FOLD))
-        ret_snd[1, pl.ds(b, GROUP)] = total.astype(BF16).reshape(GROUP, BLOCK, chunk)
+        gate, up, sigma = activations(gate_ups(block(rcv, 1, b)))
+        d_hidden = joined(
+            [mm_nt(y, wd[j]) for j in range(FOLD)], [mm_nt(part, wd_tail[...]) for part in tails_of(y)])
+        both = jnp.concatenate(cotangents(d_hidden, gate, up, sigma), axis=1)
+        total = sum(mm_nt(spread(both.astype(F32), j), wgu[j]) for j in range(FOLD))
+        ret_snd[1, pl.ds(b, GROUP)] = answer_with(total, mm_nt(both, wgu_tail[...]))
 
     for k in order:
         send_copy(0, k).wait_recv()
@@ -282,9 +308,14 @@
     all_cots = rcv3[:, count3:2 * count3, :].reshape(ne * count3, span)
     factors = fac_rcv[...].reshape(ne * count3, 3 * h)
     pair = mm_tn(all_rows, factors[:, 0:2 * h]).astype(BF16)
-    grads[0] = pair[:, 0:h]
-    grads[1] = pair[:, h:2 * h]
-    grads[2] = mm_tn(all_cots, factors[:, 2 * h:3 * h]).astype(BF16)
+    grads_buf[0] = pair[:, 0:h]
+    grads_buf[1] = pair[:, h:2 * h]
+    grads_buf[2] = mm_tn(all_cots, factors[:, 2 * h:3 * h]).astype(BF16)
+
+    stores = [
+        pltpu.make_async_copy(source, target, out_sem.at[i])
+        for i, (source, target) in enumerate(((grads_buf, grads), (out1_buf, out1), (dx2_buf, dx2)))]
+    stores[0].start()
 
     for u in (1, 2):
         for k in order:
@@ -296,34 +327,37 @@
     own_ret(1).start()
 
     back = n * BLOCK
-    first, second, back_chunk = slots(rt1[...], back, slices)
+    first, second, masks = slots(rt1[...], back, slices)
     weight = jnp.where(first, gt1[0:1, :], 0.0) + jnp.where(second, gt1[1:2, :], 0.0)
     pieces = []
-    for j in range(FOLD):
-        rest = jnp.where(back_chunk == j, weight, 0.0)
+    for mask in masks:
+        rest = jnp.where(mask, weight, 0.0)
         split = []
         for _ in range(3):
             split.append(rest.astype(BF16))
             rest = rest - split[-1].astype(F32)
         pieces.append(jnp.concatenate([turned(piece) for piece in split], axis=0))
-    first, second, back_chunk = slots(rt2[...], back, slices)
-    picked = [turned(ones((first | second) & (back_chunk == j))) for j in range(FOLD)]
+    first, second, masks = slots(rt2[...], back, slices)
+    picked = [turned(ones((first | second) & mask)) for mask in masks]
+
+    def unpacked(weights, answer):
+        yield from ((at, size, mm(weights[j], answer)) for j, (at, size) in enumerate(spans))
+        yield cut, tail, sum(mm(weights[FOLD + c], part) for c, part in enumerate(tails_of(answer)))
 
     for k in order:
         ret_copy(0, k).wait_recv()
     own_ret(0).wait()
-    answer = ret_rcv[0].reshape(back, chunk)
-    for j, (at, size) in enumerate(spans):
-        result = mm(pieces[j], answer[:, 0:size])
-        out1[:, at:at + size] = (
+    for at, size, result in unpacked(pieces, ret_rcv[0].reshape(back, chunk)):
+        out1_buf[:, at:at + size] = (
             result[0:BLOCK] + result[BLOCK:2 * BLOCK] + result[2 * BLOCK:3 * BLOCK]).astype(BF16)
+    stores[1].start()
 
     for k in order:
         ret_copy(1, k).wait_recv()
     own_ret(1).wait()
-    answer = ret_rcv[1].reshape(back, chunk)
-    for j, (at, size) in enumerate(spans):
-        dx2[:, at:at + size] = mm(picked[j], answer[:, 0:size]).astype(BF16)
+    for at, size, result in unpacked(picked, ret_rcv[1].reshape(back, chunk)):
+        dx2_buf[:, at:at + size] = result.astype(BF16)
+    stores[2].start()
 
     for k in order:
         for u in range(3):
@@ -333,6 +367,8 @@
     for k in range(1, ne):
         rows_copy(k).wait_send()
         factor_copy(k).wait_send()
+    for copy in stores:
+        copy.wait()
 
 
 def store(a, b, c, a_out, b_out, c_out, sem):
@@ -353,8 +389,8 @@
     count3 = args[7].shape[0]
     h = args[9].shape[1]
     span = depth // ne
-    chunk = -(-depth // (FOLD * 128)) * 128
-    vmem = pl.BlockSpec(memory_space=pltpu.VMEM)
+    chunk = depth // (FOLD * 128) * 128
+    tail = depth - FOLD * chunk
     hbm = pl.BlockSpec(memory_space=pl.ANY)
     results = (
             jax.ShapeDtypeStruct((tokens, depth), BF16),
@@ -365,12 +401,17 @@
         functools.partial(kernel, n, ne),
         out_shape=results,
         in_specs=[hbm] * 12,
-        out_specs=(vmem, vmem, vmem),
+        out_specs=(hbm,) * 3,
         scratch_shapes=[pltpu.VMEM(arg.shape, arg.dtype) for arg in args[:9]] + [
             pltpu.SemaphoreType.DMA((9,)),
+            pltpu.VMEM((tokens, depth), BF16),
+            pltpu.VMEM((tokens, depth), BF16),
+            pltpu.VMEM((3, span, h), BF16),
+            pltpu.SemaphoreType.DMA((3,)),
+            pltpu.VMEM((tail, 2 * h), BF16),
+            pltpu.VMEM((h, tail), BF16),
             pltpu.VMEM((FOLD, chunk, 2 * h), BF16),
             pltpu.VMEM((FOLD, h, chunk), BF16),
-            pltpu.VMEM((FOLD * BLOCK, chunk), BF16),
             pltpu.VMEM((3, EXPERTS, BLOCK, chunk), BF16),
             pltpu.VMEM((3, n, BLOCK, chunk), BF16),
             pltpu.VMEM((2, n, BLOCK, chunk), BF16),
@@ -379,7 +420,7 @@
             pltpu.VMEM((ne, 2 * count3, span), BF16),
             pltpu.VMEM((count3, 3 * h), BF16),
             pltpu.VMEM((ne, count3, 3 * h), BF16),
-            pltpu.SemaphoreType.DMA((3 * FOLD,)),
+            pltpu.SemaphoreType.DMA((3 * FOLD + 3,)),
             pltpu.SemaphoreType.DMA((7,)),
             pltpu.SemaphoreType.DMA((3, n)),
             pltpu.SemaphoreType.DMA((3, n)),
@@ -394,9 +435,10 @@
     out_one, dx_two, grads = pl.pallas_call(
         store,
         out_shape=results,
-        in_specs=[vmem] * 3,
+        in_specs=[hbm] * 3,
         out_specs=(hbm,) * 3,
         scratch_shapes=[pltpu.SemaphoreType.DMA((3,))],
+        compiler_params=pltpu.CompilerParams(vmem_limit_bytes=62 * 2**20),
     )(*landed)
     return out_one, dx_two, jnp.transpose(grads, (1, 0, 2))
 

time: 45.6 us -> 69.8 us (1.53)
  Pallas kernels: 44.8 us -> 69 us
    pallas_call x1, Pallas kernels: 2.17 us -> 28.9 us  [shards(): pl.pallas_call(store, out_shape=results, in_specs=[hbm] * 3, out_specs=(h...]
    pallas_call x1, Pallas kernels: 42.6 us -> 40.1 us  [shards(): pl.pallas_call(functools.partial(kernel, n, ne), out_shape=results, in_sp...]
where the time goes in v3:
time: 69.8 us; the launch traced here: 69.7 us
  Pallas kernels  69 us (99%)
    pallas_call x1, Pallas kernels, shards(): pl.pallas_call(functools.partial(kernel, n, ne), out_shape=results, in_sp...  40.1 us
    pallas_call x1, Pallas kernels, shards(): pl.pallas_call(store, out_shape=results, in_specs=[hbm] * 3, out_specs=(h...  28.9 us

profile of v3, /device:TPU:0, one launch (start us, length us, event | category | flops | bytes accessed | tf_op | source)
XLA Modules:
  0.0 69.7 jit_solution(8055258332430985222)
XLA Ops:
  0.6 40.1 %shard_map.139 = (bf16[16,3584]{1,0:T(8,128)(2,1)}, bf16[16,3584]{1,0:T(8,128)(2,1)}, bf16[3,896,128]{2,1,0:T(8,128)(2,1)}) custom-call(bf16[16,3584]{1,0:T(8,128)(2,1)} %tok1_hbm.1, s32[2,16]{1,0:T(2,128)} %bitcast.5, f32[2,16]{1,0:T(2,128)} %bitcast.6, bf16[16,3584]{1,0:T(8,128)(2,1)} %tok2_hbm.1, s32[2,16]{1,0:T(2,128)} %bitcast.7, f32[2,16]{1,0:T(2,128)} %bitcast.8, ...), custom_call_target="tpu_custom_call" | custom-call | tf_op jit(solution)/shard_map/pallas_call | solution.py:400
  40.7 28.9 %shard_map.140 = (bf16[16,3584]{1,0:T(8,128)(2,1)}, bf16[16,3584]{1,0:T(8,128)(2,1)}, bf16[3,896,128]{2,1,0:T(8,128)(2,1)}) custom-call(bf16[16,3584]{1,0:T(8,128)(2,1)} %get-tuple-element.9.a, bf16[16,3584]{1,0:T(8,128)(2,1)} %get-tuple-element.10.b, bf16[3,896,128]{2,1,0:T(8,128)(2,1)} %get-tuple-element.11.c), custom_call_target="tpu_custom_call" | custom-call | tf_op jit(solution)/shard_map/pallas_call | solution.py:435

commit v4 on v3

--- a/solution.py
+++ b/solution.py
@@ -172,7 +172,7 @@
     pack(0, first_one | second_one, pieces_one, tok1, None)
 
     pl.semaphore_wait(barrier, n + ne - 2)
-    order = list(range(1, n))
+    order = sorted(range(1, n), key=lambda k: abs(2 * k - n))
     for k in order:
         send_copy(0, k).start()
     own_copy(0).start()
@@ -371,14 +371,18 @@
         copy.wait()
 
 
-def store(a, b, c, a_out, b_out, c_out, sem):
-    copies = [
-        pltpu.make_async_copy(source, target, sem.at[i])
-        for i, (source, target) in enumerate(((a, a_out), (b, b_out), (c, c_out)))]
-    for copy in copies:
-        copy.start()
-    for copy in copies:
-        copy.wait()
+def store(a, b, c, a_out, b_out, c_out, a_buf, b_buf, c_buf, in_sem, out_sem):
+    triples = [(c.at[i], c_buf.at[i], c_out.at[i]) for i in range(c.shape[0])]
+    triples += [(a, a_buf, a_out), (b, b_buf, b_out)]
+    loads = [pltpu.make_async_copy(t[0], t[1], in_sem.at[i]) for i, t in enumerate(triples)]
+    saves = [pltpu.make_async_copy(t[1], t[2], out_sem.at[i]) for i, t in enumerate(triples)]
+    for load in loads:
+        load.start()
+    for load, save in zip(loads, saves):
+        load.wait()
+        save.start()
+    for save in saves:
+        save.wait()
 
 
 def shards(*args):
@@ -437,7 +441,8 @@
         out_shape=results,
         in_specs=[hbm] * 3,
         out_specs=(hbm,) * 3,
-        scratch_shapes=[pltpu.SemaphoreType.DMA((3,))],
+        scratch_shapes=[pltpu.VMEM(result.shape, result.dtype) for result in results]
+        + [pltpu.SemaphoreType.DMA((5,)), pltpu.SemaphoreType.DMA((5,))],
         compiler_params=pltpu.CompilerParams(vmem_limit_bytes=62 * 2**20),
     )(*landed)
     return out_one, dx_two, jnp.transpose(grads, (1, 0, 2))

time: 69.8 us -> 43.9 us (0.63)
  Pallas kernels: 69 us -> 43.1 us
    pallas_call x1, Pallas kernels: 28.9 us -> 2.01 us  [shards(): pl.pallas_call(store, out_shape=results, in_specs=[hbm] * 3, out_specs=(h...]
    pallas_call x1, Pallas kernels: 40.1 us -> 41.1 us  [shards(): pl.pallas_call(functools.partial(kernel, n, ne), out_shape=results, in_sp...]
where the time goes in v4:
time: 43.9 us; the launch traced here: 43.7 us
  Pallas kernels  43.1 us (98%)
  between operations  0.64 us (1%)
    pallas_call x1, Pallas kernels, shards(): pl.pallas_call(functools.partial(kernel, n, ne), out_shape=results, in_sp...  41.1 us
    pallas_call x1, Pallas kernels, shards(): pl.pallas_call(store, out_shape=results, in_specs=[hbm] * 3, out_specs=(h...  2.01 us

profile of v4, /device:TPU:0, one launch (start us, length us, event | category | flops | bytes accessed | tf_op | source)
XLA Modules:
  0.0 43.7 jit_solution(2128869434773544175)
XLA Ops:
  0.6 41.1 %shard_map.139 = (bf16[16,3584]{1,0:T(8,128)(2,1)}, bf16[16,3584]{1,0:T(8,128)(2,1)}, bf16[3,896,128]{2,1,0:T(8,128)(2,1)}) custom-call(bf16[16,3584]{1,0:T(8,128)(2,1)} %tok1_hbm.1, s32[2,16]{1,0:T(2,128)} %bitcast.5, f32[2,16]{1,0:T(2,128)} %bitcast.6, bf16[16,3584]{1,0:T(8,128)(2,1)} %tok2_hbm.1, s32[2,16]{1,0:T(2,128)} %bitcast.7, f32[2,16]{1,0:T(2,128)} %bitcast.8, ...), custom_call_target="tpu_custom_call" | custom-call | tf_op jit(solution)/shard_map/pallas_call | solution.py:404
  41.7 2.0 %shard_map.140 = (bf16[16,3584]{1,0:T(8,128)(2,1)}, bf16[16,3584]{1,0:T(8,128)(2,1)}, bf16[3,896,128]{2,1,0:T(8,128)(2,1)}) custom-call(bf16[16,3584]{1,0:T(8,128)(2,1)} %get-tuple-element.9.a, bf16[16,3584]{1,0:T(8,128)(2,1)} %get-tuple-element.10.b, bf16[3,896,128]{2,1,0:T(8,128)(2,1)} %get-tuple-element.11.c), custom_call_target="tpu_custom_call" | custom-call | tf_op jit(solution)/shard_map/pallas_call | solution.py:439

commit v5 on v4

--- a/solution.py
+++ b/solution.py
@@ -166,21 +166,12 @@
         snd[u] = with_tails(total, tails).astype(BF16).reshape(EXPERTS, BLOCK, chunk)
 
     width = EXPERTS * BLOCK
-    inputs[0].wait()
-    first_one, second_one, pieces_one = slots(rt1[...], width, 1)
-    inputs[1].wait()
-    pack(0, first_one | second_one, pieces_one, tok1, None)
-
-    pl.semaphore_wait(barrier, n + ne - 2)
-    order = sorted(range(1, n), key=lambda k: abs(2 * k - n))
-    for k in order:
-        send_copy(0, k).start()
-    own_copy(0).start()
-
-    for load in inputs[2:]:
+    for load in inputs:
         load.wait()
     first_two, second_two, pieces_two = slots(rt2[...], width, 1)
     pack(1, first_two | second_two, pieces_two, tok2, None)
+    pl.semaphore_wait(barrier, n + ne - 2)
+    order = sorted(range(1, n), key=lambda k: abs(2 * k - n))
     for k in order:
         send_copy(1, k).start()
     own_copy(1).start()
@@ -191,6 +182,13 @@
     for k in order:
         send_copy(2, k).start()
     own_copy(2).start()
+
+    first_one, second_one, pieces_one = slots(rt1[...], width, 1)
+    pack(0, first_one | second_one, pieces_one, tok1, None)
+
+    for k in order:
+        send_copy(0, k).start()
+    own_copy(0).start()
 
     count3 = rows3.shape[0]
     for j in range(ne):
@@ -291,6 +289,15 @@
         total = sum(mm_nt(spread(both.astype(F32), j), wgu[j]) for j in range(FOLD))
         ret_snd[1, pl.ds(b, GROUP)] = answer_with(total, mm_nt(both, wgu_tail[...]))
 
+    for u in (1, 2):
+        for k in order:
+            send_copy(u, k).wait_recv()
+        own_copy(u).wait()
+    groups(backward)
+    for k in order:
+        ret_copy(1, k).start()
+    own_ret(1).start()
+
     for k in order:
         send_copy(0, k).wait_recv()
     own_copy(0).wait()
@@ -316,15 +323,6 @@
         pltpu.make_async_copy(source, target, out_sem.at[i])
         for i, (source, target) in enumerate(((grads_buf, grads), (out1_buf, out1), (dx2_buf, dx2)))]
     stores[0].start()
-
-    for u in (1, 2):
-        for k in order:
-            send_copy(u, k).wait_recv()
-        own_copy(u).wait()
-    groups(backward)
-    for k in order:
-        ret_copy(1, k).start()
-    own_ret(1).start()
 
     back = n * BLOCK
     first, second, masks = slots(rt1[...], back, slices)
@@ -345,19 +343,19 @@
         yield cut, tail, sum(mm(weights[FOLD + c], part) for c, part in enumerate(tails_of(answer)))
 
     for k in order:
+        ret_copy(1, k).wait_recv()
+    own_ret(1).wait()
+    for at, size, result in unpacked(picked, ret_rcv[1].reshape(back, chunk)):
+        dx2_buf[:, at:at + size] = result.astype(BF16)
+    stores[2].start()
+
+    for k in order:
         ret_copy(0, k).wait_recv()
     own_ret(0).wait()
     for at, size, result in unpacked(pieces, ret_rcv[0].reshape(back, chunk)):
         out1_buf[:, at:at + size] = (
             result[0:BLOCK] + result[BLOCK:2 * BLOCK] + result[2 * BLOCK:3 * BLOCK]).astype(BF16)
     stores[1].start()
-
-    for k in order:
-        ret_copy(1, k).wait_recv()
-    own_ret(1).wait()
-    for at, size, result in unpacked(picked, ret_rcv[1].reshape(back, chunk)):
-        dx2_buf[:, at:at + size] = result.astype(BF16)
-    stores[2].start()
 
     for k in order:
         for u in range(3):

time: 43.9 us -> 44.1 us (level)
  no operation moved by 1% of the time
where the time goes in v5:
time: 44.1 us; the launch traced here: 43.9 us
  Pallas kernels  43.3 us (98%)
  between operations  0.64 us (1%)
    pallas_call x1, Pallas kernels, shards(): pl.pallas_call(functools.partial(kernel, n, ne), out_shape=results, in_sp...  41.3 us
    pallas_call x1, Pallas kernels, shards(): pl.pallas_call(store, out_shape=results, in_specs=[hbm] * 3, out_specs=(h...  2.01 us

profile of v5, /device:TPU:0, one launch (start us, length us, event | category | flops | bytes accessed | tf_op | source)
XLA Modules:
  0.0 43.9 jit_solution(10100942157315618663)
XLA Ops:
  0.6 41.3 %shard_map.139 = (bf16[16,3584]{1,0:T(8,128)(2,1)}, bf16[16,3584]{1,0:T(8,128)(2,1)}, bf16[3,896,128]{2,1,0:T(8,128)(2,1)}) custom-call(bf16[16,3584]{1,0:T(8,128)(2,1)} %tok1_hbm.1, s32[2,16]{1,0:T(2,128)} %bitcast.5, f32[2,16]{1,0:T(2,128)} %bitcast.6, bf16[16,3584]{1,0:T(8,128)(2,1)} %tok2_hbm.1, s32[2,16]{1,0:T(2,128)} %bitcast.7, f32[2,16]{1,0:T(2,128)} %bitcast.8, ...), custom_call_target="tpu_custom_call" | custom-call | tf_op jit(solution)/shard_map/pallas_call | solution.py:402
  41.9 2.0 %shard_map.140 = (bf16[16,3584]{1,0:T(8,128)(2,1)}, bf16[16,3584]{1,0:T(8,128)(2,1)}, bf16[3,896,128]{2,1,0:T(8,128)(2,1)}) custom-call(bf16[16,3584]{1,0:T(8,128)(2,1)} %get-tuple-element.9.a, bf16[16,3584]{1,0:T(8,128)(2,1)} %get-tuple-element.10.b, bf16[3,896,128]{2,1,0:T(8,128)(2,1)} %get-tuple-element.11.c), custom_call_target="tpu_custom_call" | custom-call | tf_op jit(solution)/shard_map/pallas_call | solution.py:437
